TPU v7x, 32 devices: a whole 2x2x4 slice. The times are simulated.
32 devices in a mesh: groups: 2 (over y), wide: 8 (over z, x), short: 2 (over core).
Axes of the slice: x: 2, y: 2, z: 4, core: 2. Of those that a mesh axis runs over, the one named last changes fastest.
Arguments:
- tokens: bfloat16 [64, 5120], P(('groups', 'wide'), 'short'), parts along dimension 0, may hold values from -6 to 6
- norm_gain: float32 [5120], P('short'), may hold values from 0.5 to 1.5
- mixer_in: bfloat16 [5120, 2, 5888], P('short', None, 'wide'), may hold values from -0.078125 to 0.078125
- shared_in: bfloat16 [5120, 512], P('short', 'wide'), may hold values from -0.078125 to 0.078125
- step_in: bfloat16 [5120, 32], P('short'), may hold values from -0.078125 to 0.078125
- step_bias: float32 [32], P('short'), may hold values from -2 to 1
- decay_rate: float32 [32], P('short'), may hold values from 0.05 to 4
- skip_gain: float32 [32], P('short'), may hold values from 0.2 to 1.5
- cached_keys: bfloat16 [16, 512, 512], P(('groups', 'wide'), None, 'short'), parts along dimension 0, may hold values from -64 to 64
- cached_values: bfloat16 [16, 512, 512], P(('groups', 'wide'), None, 'short'), parts along dimension 0, may hold values from -6 to 6
- lengths: int32 [16], P(('groups', 'wide')), parts along dimension 0, may hold values from 2 to 512, as said below
- state_cache: bfloat16 [16, 32, 128, 256], P(('groups', 'wide'), 'short'), parts along dimension 0, may hold values from -6 to 6
- mixer_gain: float32 [4096], P('short'), may hold values from 0.5 to 1.5
- mixer_out: bfloat16 [2, 3328, 5120], P(None, 'wide', 'short'), may hold values from -0.078125 to 0.078125
- gate_weight: bfloat16 [5120, 21504], P('short', 'wide'), may hold values from -0.078125 to 0.078125
- up_weight: bfloat16 [5120, 21504], P('short', 'wide'), may hold values from -0.078125 to 0.078125
- down_weight: bfloat16 [21504, 5120], P('wide', 'short'), may hold values from -0.0390625 to 0.0390625
Outputs:
- mixed: bfloat16 [64, 5120], P(('groups', 'wide'), 'short'), parts along dimension 0
There are 2 independent parts, one for each index of `groups`. A program takes and returns all parts, laid end to end along the dimension named above; an argument that names none is the same for every part. Nothing has to cross between parts.
Inputs may be any that keep to these rules, and one draw needn't show every extreme that they name: `lengths`: in every draw some request holds exactly 512 earlier tokens.
All inputs are finite; a program needn't handle non-finite values.
Results may differ from a plain program's by a relative error of at most 0.009.
Values may be sent and summed in bfloat16 or wider, within the bound.
No kernel may reach another device: no remote copies, remote signals or barrier semaphores. Data moves between devices by JAX's collectives and lax.ppermute only.
A program may use at most 128 MiB of HBM per device.

v0:
```python
import jax
import jax.numpy as jnp
from jax import lax
from jax.sharding import PartitionSpec as P

D = 5120
QUERY_HEADS = 20
KEY_VALUE_HEADS = 4
HEAD_SIZE = 128
MH = 32
MP = 128
NS = 256
CACHE_SLOTS = 512
DRAFT_TOKENS = 4


epsilon = 1e-05


def as_sent(x):

    def short(part):
        return part.astype(jnp.bfloat16) if part.dtype == jnp.float32 else part

    return jax.tree.map(short, x)


def rotate(vectors, cos_table, sin_table):
    half_width = vectors.shape[-1] // 2
    first_half = vectors[..., :half_width]
    second_half = vectors[..., half_width:]
    return jnp.concatenate(
        [
            first_half * cos_table - second_half * sin_table,
            second_half * cos_table + first_half * sin_table,
        ],
        axis=-1,
    )


def rope_tables(positions):
    frequency = 10000.0 ** (-(jnp.arange(HEAD_SIZE // 2, dtype=jnp.float32) * 2.0 / HEAD_SIZE))
    angles = positions.astype(jnp.float32)[..., None] * frequency
    return (jnp.cos(angles), jnp.sin(angles))


def attend_one(queries, fresh_keys, fresh_values, key_tile_block, value_tile_block, length):
    score_scale = HEAD_SIZE ** (-0.5)
    scores_cache = (
        jnp.einsum("tkgd,pkd->kgtp", queries, key_tile_block, preferred_element_type=jnp.float32)
        * score_scale
    )
    scores_new = (
        jnp.einsum("tkgd,ukd->kgtu", queries, fresh_keys, preferred_element_type=jnp.float32)
        * score_scale
    )
    live_keys = jnp.arange(key_tile_block.shape[0], dtype=jnp.int32) < length
    causal = jnp.arange(DRAFT_TOKENS)[None, :] <= jnp.arange(DRAFT_TOKENS)[:, None]
    scores_cache = jnp.where(live_keys, scores_cache, -1e30)
    scores_new = jnp.where(causal, scores_new, -1e30)
    highest = jnp.maximum(jnp.max(scores_cache, axis=-1), jnp.max(scores_new, axis=-1))[..., None]
    weight_cache = jnp.exp(scores_cache - highest)
    weight_new = jnp.exp(scores_new - highest)
    denominator = jnp.sum(weight_cache, axis=-1, keepdims=True) + jnp.sum(
        weight_new, axis=-1, keepdims=True
    )
    probs_cache = (weight_cache / denominator).astype(jnp.bfloat16)
    probs_new = (weight_new / denominator).astype(jnp.bfloat16)
    attended = jnp.einsum(
        "kgtp,pkd->tkgd", probs_cache, value_tile_block, preferred_element_type=jnp.float32
    )
    attended = attended + jnp.einsum(
        "kgtu,ukd->tkgd", probs_new, fresh_values, preferred_element_type=jnp.float32
    )
    return attended.astype(jnp.bfloat16)


def scan_one(
    state_block, inputs_x, gates_z, b_vals, c_vals, step_sizes, decay_rates, skip_gain, head_gain
):
    hstate = state_block.astype(jnp.float32)
    in_active = jax.nn.silu(inputs_x.astype(jnp.float32))
    write_vec = jax.nn.silu(b_vals.astype(jnp.float32))
    read_vec = jax.nn.silu(c_vals.astype(jnp.float32))
    outputs = []
    for draft_index in range(DRAFT_TOKENS):
        decays = jnp.exp(-step_sizes[draft_index] * decay_rates)
        inject = (step_sizes[draft_index][:, None] * in_active[draft_index])[
            :, :, None
        ] * write_vec[draft_index][None, None, :]
        hstate = decays[:, None, None] * hstate + inject
        readout = jnp.einsum(
            "hpn,n->hp", hstate, read_vec[draft_index], precision=lax.Precision.HIGHEST
        )
        outputs.append(readout + skip_gain[:, None] * in_active[draft_index])
    gated = jnp.stack(outputs) * jax.nn.silu(gates_z.astype(jnp.float32))
    mean_square = jnp.mean(gated * gated, axis=-1, keepdims=True)
    return (gated * lax.rsqrt(mean_square + epsilon) * head_gain).astype(jnp.bfloat16)


def on_device(
    tokens,
    norm_gain,
    mixer_in,
    shared_in,
    step_in,
    step_bias,
    decay_rate,
    skip_gain,
    cached_keys,
    cached_values,
    lengths,
    state_cache,
    mixer_gain,
    mixer_out,
    gate_weight,
    up_weight,
    down_weight,
):
    short_count = lax.axis_size("short")
    n_wide = lax.axis_size("wide")
    q_heads = QUERY_HEADS // short_count
    key_value_heads = KEY_VALUE_HEADS // short_count
    ssm_heads = MH // short_count
    repeat_factor = QUERY_HEADS // KEY_VALUE_HEADS
    query_size = q_heads * HEAD_SIZE
    key_size = key_value_heads * HEAD_SIZE
    m_size = ssm_heads * MP
    local_rows = tokens.shape[0]
    requests = local_rows // DRAFT_TOKENS
    width_half = tokens.shape[1]
    rows_float = tokens.astype(jnp.float32)
    square_sum = lax.psum(jnp.sum(rows_float * rows_float, axis=1), "short")
    inv_rms = lax.rsqrt(square_sum / D + epsilon)
    normed = (rows_float * inv_rms[:, None] * norm_gain[None, :]).astype(jnp.bfloat16)
    step_terms = jnp.dot(normed, step_in, preferred_element_type=jnp.float32)
    step_raw = lax.psum_scatter(step_terms, "short", scatter_dimension=1, tiled=True)
    gathered = lax.all_gather(normed, "wide", axis=0, tiled=True)
    group_part = jnp.einsum("rd,dgc->rgc", gathered, mixer_in, preferred_element_type=jnp.float32)
    shared_part = jnp.dot(gathered, shared_in, preferred_element_type=jnp.float32)[:, None, :]
    gate_part = jnp.dot(gathered, gate_weight, preferred_element_type=jnp.float32)
    up_part = jnp.dot(gathered, up_weight, preferred_element_type=jnp.float32)
    gate_half, up_half = (
        lax.psum_scatter(
            gate_part.astype(jnp.bfloat16), "short", scatter_dimension=0, tiled=True
        ).astype(jnp.float32),
        lax.psum_scatter(
            up_part.astype(jnp.bfloat16), "short", scatter_dimension=0, tiled=True
        ).astype(jnp.float32),
    )
    hidden_half = (jax.nn.silu(gate_half) * up_half).astype(jnp.bfloat16)
    hidden = lax.all_gather(hidden_half, "short", axis=0, tiled=True)
    group_moved, shared_moved = (
        lax.all_to_all(group_part, "wide", split_axis=0, concat_axis=2, tiled=True),
        lax.all_to_all(shared_part, "wide", split_axis=0, concat_axis=2, tiled=True),
    )
    group_sum = lax.psum_scatter(group_moved, "short", scatter_dimension=1, tiled=True)
    shared_sum = lax.psum(shared_moved, "short")
    features = group_sum[:, 0, :].astype(jnp.bfloat16)
    shared_vals = shared_sum[:, 0, :].astype(jnp.bfloat16)
    queries = features[:, :query_size].reshape(requests, DRAFT_TOKENS, q_heads, HEAD_SIZE)
    fresh_keys = features[:, query_size : query_size + key_size].reshape(
        requests, DRAFT_TOKENS, key_value_heads, HEAD_SIZE
    )
    fresh_values = features[:, query_size + key_size : query_size + 2 * key_size].reshape(
        requests, DRAFT_TOKENS, key_value_heads, HEAD_SIZE
    )
    x_start = query_size + 2 * key_size
    inputs_x = features[:, x_start : x_start + m_size].reshape(
        requests, DRAFT_TOKENS, ssm_heads, MP
    )
    gates_z = features[:, x_start + m_size : x_start + 2 * m_size].reshape(
        requests, DRAFT_TOKENS, ssm_heads, MP
    )
    positions = lengths[:, None] + jnp.arange(DRAFT_TOKENS, dtype=jnp.int32)[None, :]
    cos_table, sin_table = rope_tables(positions)
    cos_table = cos_table[:, :, None, :]
    sin_table = sin_table[:, :, None, :]
    rotated_queries = rotate(queries.astype(jnp.float32), cos_table, sin_table).astype(jnp.bfloat16)
    keys_rot = rotate(fresh_keys.astype(jnp.float32), cos_table, sin_table).astype(jnp.bfloat16)
    rotated_queries = rotated_queries.reshape(
        requests, DRAFT_TOKENS, key_value_heads, repeat_factor, HEAD_SIZE
    )
    key_tile_block = cached_keys.reshape(requests, CACHE_SLOTS, key_value_heads, HEAD_SIZE)
    value_tile_block = cached_values.reshape(requests, CACHE_SLOTS, key_value_heads, HEAD_SIZE)
    attention = jax.vmap(attend_one)(
        rotated_queries, keys_rot, fresh_values, key_tile_block, value_tile_block, lengths
    )
    step_sizes = jax.nn.softplus(
        step_raw.reshape(requests, DRAFT_TOKENS, ssm_heads) + step_bias[None, None, :]
    )
    b_vals = shared_vals[:, :NS].reshape(requests, DRAFT_TOKENS, NS)
    c_vals = shared_vals[:, NS:].reshape(requests, DRAFT_TOKENS, NS)
    head_gain = mixer_gain.reshape(ssm_heads, MP)
    mamba = jax.vmap(scan_one, in_axes=(0, 0, 0, 0, 0, 0, None, None, None))(
        state_cache, inputs_x, gates_z, b_vals, c_vals, step_sizes, decay_rate, skip_gain, head_gain
    )
    own_rows = jnp.concatenate(
        [attention.reshape(local_rows, query_size), mamba.reshape(local_rows, m_size)], axis=1
    )
    returned = lax.all_to_all(
        as_sent(own_rows[:, None, :]), "wide", split_axis=2, concat_axis=0, tiled=True
    )
    both_groups = lax.all_gather(as_sent(returned), "short", axis=1, tiled=True).astype(
        returned.dtype
    )
    projected = jnp.einsum(
        "rgc,gcd->rd", both_groups, mixer_out, preferred_element_type=jnp.float32
    )
    summed = projected + jnp.dot(hidden, down_weight, preferred_element_type=jnp.float32)
    pieces = lax.all_to_all(
        summed.reshape(n_wide, local_rows, width_half).astype(jnp.bfloat16),
        "wide",
        split_axis=0,
        concat_axis=0,
        tiled=True,
    ).astype(jnp.float32)
    total = rows_float + jnp.sum(pieces, axis=0)
    return total.astype(jnp.bfloat16)


def solution(mesh):
    in_specs = (
        P(("groups", "wide"), "short"),
        P("short"),
        P("short", None, "wide"),
        P("short", "wide"),
        P("short", None),
        P("short"),
        P("short"),
        P("short"),
        P(("groups", "wide"), None, "short"),
        P(("groups", "wide"), None, "short"),
        P(("groups", "wide")),
        P(("groups", "wide"), "short", None, None),
        P("short"),
        P(None, "wide", "short"),
        P("short", "wide"),
        P("short", "wide"),
        P("wide", "short"),
    )
    out_specs = P(("groups", "wide"), "short")
    return jax.shard_map(
        on_device, mesh=mesh, in_specs=in_specs, out_specs=out_specs, check_vma=False
    )
```

profile of v0, /device:TPU:0, one launch (start us, length us, event | category | flops | bytes accessed | tf_op | source)
XLA Modules:
  0.0 175.8 jit_solution(5876749389254881673)
XLA Ops:
  7.4 2.6 %psum.14 = f32[4]{0:T(128)S(1)} all-reduce(f32[4]{0:T(128)S(1)} %fusion.60), channel_id=1, replica_groups=mesh['groups'=2,'wide'=8,'short'=2] {'short'}, use_global_device_ids=true, to_apply=%region_1.0 | all-reduce | flops 4 | bytes 32 | tf_op jit(solution)/shard_map/psum | solution.py:133
  10.9 32.2 %all-gather = bf16[8,4,2560]{2,1,0:T(4,128)(2,1)S(1)} all-gather(bf16[1,4,2560]{2,1,0:T(4,128)(2,1)S(1)} %fusion.99), channel_id=1, replica_groups=mesh['groups'=2,'wide'=8,'short'=2] {'wide'}, dimensions={0}, use_global_device_ids=true | all-gather | bytes 184320 | tf_op jit(solution)/shard_map/all_gather | solution.py:138
  45.3 5.5 %all-to-all-start.1 = ((f32[8,1,256]{2,1,0:T(1,128)}), f32[8,1,256]{2,1,0:T(1,128)S(1)}, u32[]{:S(2)}, u32[]{:S(2)}) async-start(f32[8,1,256]{2,1,0:T(1,128)} %reshape.648), calls=%async_computation.1 | async-start | bytes 16384 | tf_op jit(solution)/shard_map/all_to_all | solution.py:155
  50.8 1.8 %convolution_bitcast_fusion.2 = f32[32,4]{1,0:T(8,128)} fusion(bf16[2560,32]{0,1:T(8,128)(2,1)} %param.21, bf16[4,2560]{1,0:T(4,128)(2,1)} %param.17, f32[2560]{0:T(1024)} %param.18, f32[4]{0:T(128)S(1)} %add_rsqrt_fusion.1), kind=kOutput, calls=%fused_computation.27 | convolution fusion | flops 696320 | bytes 195088
  52.7 8.0 %convolution_convert_fusion.1 = bf16[32,2688]{1,0:T(8,128)(2,1)} fusion(bf16[32,2560]{1,0:T(8,128)(2,1)S(1)} %reshape.629, bf16[2560,2688]{1,0:T(8,128)(2,1)} %param.31), kind=kOutput, calls=%fused_computation.4 | convolution fusion | flops 440487936 | bytes 14098432 | tf_op jit(solution)/shard_map/dot_general | solution.py:141
  60.8 8.0 %convolution_convert_fusion = bf16[32,2688]{1,0:T(8,128)(2,1)} fusion(bf16[32,2560]{1,0:T(8,128)(2,1)S(1)} %reshape.629, bf16[2560,2688]{1,0:T(8,128)(2,1)} %param.32), kind=kOutput, calls=%fused_computation.3 | convolution fusion | flops 440487936 | bytes 14098432 | tf_op jit(solution)/shard_map/dot_general | solution.py:142
  69.0 5.4 %fusion.103 = f32[32,2,736]{2,0,1:T(8,128)S(1)} fusion(bf16[32,2560,1]{1,0,2:T(8,128)(2,1)S(1)} %reshape.630, bf16[2560,2,736]{0,2,1:T(8,128)(2,1)} %param.19), kind=kOutput, calls=%fused_computation.182 | convolution fusion | flops 241172480 | bytes 7888896 | tf_op jit(solution)/shard_map/rd,dgc->rgc/dot_general | solution.py:139
  77.6 6.1 %all-to-all-start = ((f32[32,2,736]{2,1,0:T(2,128)}), f32[32,2,736]{2,1,0:T(2,128)S(1)}, u32[]{:S(2)}, u32[]{:S(2)}) async-start(f32[32,2,736]{2,1,0:T(2,128)} %copy.63), calls=%async_computation | async-start | bytes 393216 | tf_op jit(solution)/shard_map/all_to_all | solution.py:154
  84.5 6.9 %all-to-all-done = f32[32,2,736]{2,1,0:T(2,128)S(1)} async-done(((f32[32,2,736]{2,1,0:T(2,128)}), f32[32,2,736]{2,1,0:T(2,128)S(1)}, u32[]{:S(2)}, u32[]{:S(2)}) %all-to-all-start) | async-done | bytes 188448 | tf_op jit(solution)/shard_map/all_to_all | solution.py:154
  91.8 4.2 %all-reduce.3 = (bf16[4,2,5888]{2,0,1:T(4,128)(2,1)S(1)}, bf16[4,1,512]{2,0,1:T(4,128)(2,1)S(1)}) all-reduce(f32[4,2,5888]{2,0,1:T(4,128)S(1)} %copy.65, f32[4,1,512]{2,0,1:T(4,128)S(1)} %all_to_all.49), channel_id=2, replica_groups=mesh['groups'=2,'wide'=8,'short'=2] {'short'}, use_global_device_ids=true, to_apply=%region_2.0.clone | all-reduce | flops 49152 | bytes 294912
  98.3 2.2 %fusion.7 = f32[1,16,128]{2,0,1:T(1,128)S(1)} fusion(bf16[1,16,128,256]{3,2,1,0:T(8,128)(2,1)S(1)} %copy-done.8, f32[256]{0:T(256)S(1)} %bitcast.286, f32[16,128]{1,0:T(8,128)S(1)} %get-tuple-element.15, f32[16]{0:T(128)S(1)} %get-tuple-element.27, f32[1,4,256]{2,1,0:T(4,128)S(1)} %get-tuple-element.21), kind=kOutput, calls=%fused_computation.11 | convolution fusion | flops 8388608 | bytes 1067520 | tf_op jit(solution)/shard_map/vmap(hpn,n->hp)/dot_general | solution.py:92
  100.5 2.6 %fusion.5 = f32[1,16,128]{2,0,1:T(1,128)S(1)} fusion(bf16[1,16,128,256]{3,2,1,0:T(8,128)(2,1)S(1)} %copy-done.8, f32[256]{0:T(256)S(1)} %bitcast.293, f32[16,128]{1,0:T(8,128)S(1)} %get-tuple-element.18, f32[16]{0:T(128)S(1)} %get-tuple-element.28, f32[256]{0:T(256)S(1)} %bitcast.287, f32[16,128]{1,0:T(8,128)S(1)} %get-tuple-element.15, ...), kind=kOutput, calls=%fused_computation.9 | convolution fusion | flops 9961472 | bytes 1077248 | tf_op jit(solution)/shard_map/vmap(hpn,n->hp)/dot_general | solution.py:92
  103.1 2.8 %fusion.3 = f32[1,16,128]{2,0,1:T(1,128)S(1)} fusion(bf16[1,16,128,256]{3,2,1,0:T(8,128)(2,1)S(1)} %copy-done.8, f32[256]{0:T(256)S(1)} %bitcast.291, f32[16,128]{1,0:T(8,128)S(1)} %get-tuple-element.17, f32[16]{0:T(128)S(1)} %get-tuple-element.30, f32[256]{0:T(256)S(1)} %bitcast.294, f32[16,128]{1,0:T(8,128)S(1)} %get-tuple-element.18, ...), kind=kOutput, calls=%fused_computation.7 | convolution fusion | flops 11534336 | bytes 1086976 | tf_op jit(solution)/shard_map/vmap(hpn,n->hp)/dot_general | solution.py:92
  105.9 3.0 %fusion.1 = f32[1,16,128]{2,0,1:T(1,128)S(1)} fusion(bf16[1,16,128,256]{3,2,1,0:T(8,128)(2,1)S(1)} %copy-done.8, f32[256]{0:T(256)S(1)} %bitcast.290, f32[16,128]{1,0:T(8,128)S(1)} %get-tuple-element.16, f32[16]{0:T(128)S(1)} %get-tuple-element.29, f32[256]{0:T(256)S(1)} %bitcast.292, f32[16,128]{1,0:T(8,128)S(1)} %get-tuple-element.17, ...), kind=kOutput, calls=%fused_computation.5 | convolution fusion | flops 13107200 | bytes 1096704 | tf_op jit(solution)/shard_map/vmap(hpn,n->hp)/dot_general | solution.py:92
  109.3 2.4 %copy.78 = bf16[4,1,3328]{0,1,2:T(2,128)(2,1)S(1)} copy(bf16[4,1,3328]{2,0,1:T(4,128)(2,1)S(1)} %maximum_bitcast_fusion.1) | data formatting | bytes 53248 | tf_op jit(solution)/shard_map/broadcast_in_dim | solution.py:202
  112.2 18.3 %reduce.7 = bf16[3328,4]{1,0:T(8,128)(2,1)S(1)} reduce(bf16[3328,1,4]{2,1,0:T(2,128)(2,1)S(1)} %bitcast.260, bf16[]{:T(256)} %broadcast.303), dimensions={1}, to_apply=%bitcast.239.reduce_sub_computation | reduce | bytes 53250
  131.9 3.3 %all-to-all-start.2 = ((bf16[8,2,832]{2,1,0:T(2,128)(2,1)}), bf16[8,2,832]{2,1,0:T(2,128)(2,1)S(1)}, u32[]{:S(2)}, u32[]{:S(2)}) async-start(bf16[8,2,832]{2,1,0:T(2,128)(2,1)} %reshape.650), calls=%async_computation.2 | async-start | bytes 57344 | tf_op jit(solution)/shard_map/all_to_all | solution.py:201
  136.3 2.1 %all_gather.11 = bf16[32,2688]{1,0:T(8,128)(2,1)S(1)} all-gather(bf16[16,2688]{1,0:T(8,128)(2,1)S(1)} %fusion.55), channel_id=1, replica_groups=mesh['groups'=2,'wide'=8,'short'=2] {'short'}, dimensions={0}, use_global_device_ids=true | all-gather | bytes 258048 | tf_op jit(solution)/shard_map/all_gather | solution.py:152
  138.4 3.4 %all-to-all-done.2 = bf16[8,2,832]{2,1,0:T(2,128)(2,1)S(1)} async-done(((bf16[8,2,832]{2,1,0:T(2,128)(2,1)}), bf16[8,2,832]{2,1,0:T(2,128)(2,1)S(1)}, u32[]{:S(2)}, u32[]{:S(2)}) %all-to-all-start.2) | async-done | bytes 26656 | tf_op jit(solution)/shard_map/all_to_all | solution.py:201
  141.8 2.1 %reshape.651 = bf16[3328,1,4]{2,1,0:T(2,128)(2,1)S(1)} reshape(bf16[8,2,832]{2,1,0:T(2,128)(2,1)S(1)} %all-to-all-done.2) | data formatting | bytes 53248
  145.7 1.9 %all_gather.10 = bf16[32,2,416]{2,0,1:T(8,128)(2,1)S(1)} all-gather(bf16[32,1,416]{2,0,1:T(8,128)(2,1)S(1)} %all_to_all.53), channel_id=1, replica_groups=mesh['groups'=2,'wide'=8,'short'=2] {'short'}, dimensions={1}, use_global_device_ids=true | all-gather | bytes 79872 | tf_op jit(solution)/shard_map/all_gather | solution.py:204
  147.6 3.0 %convolution_bitcast_fusion = f32[32,2560]{1,0:T(8,128)S(1)} fusion(bf16[32,2,416]{2,0,1:T(8,128)(2,1)S(1)} %all_gather.10, bf16[2,416,2560]{2,1,0:T(8,128)(2,1)} %param.30), kind=kOutput, calls=%fused_computation.1 | convolution fusion | flops 136314880 | bytes 4640768 | tf_op jit(solution)/shard_map/rgc,gcd->rd/dot_general | solution.py:207
  150.6 7.4 %fusion = bf16[32,2560]{1,0:T(8,128)(2,1)S(1)} fusion(f32[32,2560]{1,0:T(8,128)S(1)} %convolution_bitcast_fusion, bf16[32,2688]{1,0:T(8,128)(2,1)S(1)} %all_gather.11, bf16[2688,2560]{1,0:T(8,128)(2,1)} %param.33), kind=kOutput, calls=%fused_computation.2 | convolution fusion | flops 440565760 | bytes 14426112 | tf_op jit(solution)/shard_map/dot_general | solution.py:210
  158.1 10.5 %all_to_all.59 = bf16[8,4,2560]{2,1,0:T(4,128)(2,1)S(1)} all-to-all(bf16[8,4,2560]{2,1,0:T(4,128)(2,1)S(1)} %convert_element_type.187), channel_id=1, replica_groups=mesh['groups'=2,'wide'=8,'short'=2] {'wide'}, dimensions={0} | all-to-all | bytes 327680 | tf_op jit(solution)/shard_map/all_to_all | solution.py:211
  (100 shorter events, 15.9 us)
Async XLA Ops:
  6.5 36.6 %copy-start = (bf16[2560,64]{0,1:T(8,128)(2,1)S(1)}, bf16[2560,64]{0,1:T(8,128)(2,1)}, u32[]{:S(2)}) copy-start(bf16[2560,64]{0,1:T(8,128)(2,1)} %param.20) | copy-start | bytes 983044
  45.3 32.3 %all-to-all-start.1 = ((f32[8,1,256]{2,1,0:T(1,128)}), f32[8,1,256]{2,1,0:T(1,128)S(1)}, u32[]{:S(2)}, u32[]{:S(2)}) async-start(f32[8,1,256]{2,1,0:T(1,128)} %reshape.648), calls=%async_computation.1 | async-start | bytes 16384 | tf_op jit(solution)/shard_map/all_to_all | solution.py:155
  50.8 26.0 %reduce-scatter.10.cloned.1.call-start = ((), (), s32[]{:S(2)}) async-start(), calls=%async_computation.9 | async-start | bytes 24576
  52.6 82.6 %reduce-scatter.6.cloned.1.call-start = ((), (), s32[]{:S(2)}) async-start(), calls=%async_computation.7 | async-start | bytes 258048 | tf_op jit(solution)/shard_map/reduce_scatter | solution.py:144
  60.7 74.6 %reduce-scatter.8.cloned.1.call-start = ((), (), s32[]{:S(2)}) async-start(), calls=%async_computation.8 | async-start | bytes 258048 | tf_op jit(solution)/shard_map/reduce_scatter | solution.py:147
  68.9 6.9 %copy-start.1 = (bf16[1,512,256]{2,1,0:T(8,128)(2,1)S(1)}, bf16[1,512,256]{2,1,0:T(8,128)(2,1)}, u32[]{:S(2)}) copy-start(bf16[1,512,256]{2,1,0:T(8,128)(2,1)} %param.25) | copy-start | bytes 786436
  68.9 7.0 %copy-start.2 = (bf16[1,512,256]{2,1,0:T(8,128)(2,1)S(1)}, bf16[1,512,256]{2,1,0:T(8,128)(2,1)}, u32[]{:S(2)}) copy-start(bf16[1,512,256]{2,1,0:T(8,128)(2,1)} %param.26) | copy-start | bytes 786436
  69.0 7.1 %copy-start.9 = (u32[32]{0:T(128)S(1)}, u32[32]{0:T(128)}, u32[]{:S(2)}) copy-start(u32[32]{0:T(128)} %constant.43) | copy-start | bytes 388
  69.0 8.6 %copy-start.6 = (f32[16]{0:T(128)S(1)}, f32[16]{0:T(128)}, u32[]{:S(2)}) copy-start(f32[16]{0:T(128)} %param.22) | copy-start | bytes 196
  69.0 14.7 %copy-start.7 = (f32[16]{0:T(128)S(1)}, f32[16]{0:T(128)}, u32[]{:S(2)}) copy-start(f32[16]{0:T(128)} %param.23) | copy-start | bytes 196
  77.5 20.8 %copy-start.8 = (bf16[1,16,128,256]{3,2,1,0:T(8,128)(2,1)S(1)}, bf16[1,16,128,256]{3,2,1,0:T(8,128)(2,1)}, u32[]{:S(2)}) copy-start(bf16[1,16,128,256]{3,2,1,0:T(8,128)(2,1)} %param.28) | copy-start | bytes 3145732
  77.6 13.9 %all-to-all-start = ((f32[32,2,736]{2,1,0:T(2,128)}), f32[32,2,736]{2,1,0:T(2,128)S(1)}, u32[]{:S(2)}, u32[]{:S(2)}) async-start(f32[32,2,736]{2,1,0:T(2,128)} %copy.63), calls=%async_computation | async-start | bytes 393216 | tf_op jit(solution)/shard_map/all_to_all | solution.py:154
  105.9 3.0 %copy-start.5 = (f32[16]{0:T(128)S(1)}, f32[16]{0:T(128)}, u32[]{:S(2)}) copy-start(f32[16]{0:T(128)} %param.24) | copy-start | bytes 196
  105.9 3.3 %copy-start.4 = (f32[2048]{0:T(1024)S(1)}, f32[2048]{0:T(1024)}, u32[]{:S(2)}) copy-start(f32[2048]{0:T(1024)} %param.29) | copy-start | bytes 24580
  131.9 9.9 %all-to-all-start.2 = ((bf16[8,2,832]{2,1,0:T(2,128)(2,1)}), bf16[8,2,832]{2,1,0:T(2,128)(2,1)S(1)}, u32[]{:S(2)}, u32[]{:S(2)}) async-start(bf16[8,2,832]{2,1,0:T(2,128)(2,1)} %reshape.650), calls=%async_computation.2 | async-start | bytes 57344 | tf_op jit(solution)/shard_map/all_to_all | solution.py:201
  150.6 18.0 %copy-start.3 = (bf16[4,2560]{1,0:T(4,128)(2,1)S(1)}, bf16[4,2560]{1,0:T(4,128)(2,1)}, u32[]{:S(2)}) copy-start(bf16[4,2560]{1,0:T(4,128)(2,1)} %param.17) | copy-start | bytes 61444
Sparse Core Ops, SparseCore 0:
  53.8 8.8 reduce-scatter.9
  64.9 8.7 reduce-scatter.5
  75.9 8.6 reduce-scatter.7
where the time goes:
time: 177 us; the launch traced here: 176 us
  blocking collectives  53.5 us (30%)
  matrix products  45.4 us (26%)
  other arithmetic  24.1 us (14%)
  starting transfers between devices  15 us (8%)
  between operations  14.2 us (8%)
  local copies, waits for them, and re-layouts  13.2 us (7%)
  waiting for transfers between devices  10.4 us (6%)
    all_gather x1, blocking collectives, on_device(): gathered = lax.all_gather(normed, 'wide', axis=0, tiled=True)  32.2 us
    unnamed x3, other arithmetic  19.2 us
    dot_general x4, matrix products, scan_one(): jnp.einsum('hpn,n->hp', hstate, read_vec[draft_index], precision=lax.Prec...  10.6 us
    all_to_all x1, blocking collectives, on_device(): lax.all_to_all(summed.reshape(n_wide, local_rows, width_half).astype(jnp....  10.5 us
    dot_general x1, matrix products, on_device(): up_part = jnp.dot(gathered, up_weight, preferred_element_type=jnp.float32)  8.04 us
    dot_general x1, matrix products, on_device(): jnp.dot(gathered, gate_weight, preferred_element_type=jnp.float32)  8.02 us
    dot_general x1, matrix products, on_device(): jnp.dot(hidden, down_weight, preferred_element_type=jnp.float32)  7.37 us
    all_to_all x1, waiting for transfers between devices, on_device(): lax.all_to_all(group_part, 'wide', split_axis=0, concat_axis=2, tiled=True)  6.92 us
  transfers between devices with their start and end apart: 6, of which 2 were waited for; matrix products, arithmetic and copies ran while one was open for 36% of the time, Pallas kernels for 0%

commit v1 on v0

v1 whole, which is shorter than its diff:
```python
import functools

import jax
import jax.numpy as jnp
from jax import lax
from jax.experimental import pallas as pl
from jax.experimental.pallas import tpu as pltpu
from jax.sharding import PartitionSpec as P

QUERY_HEADS = 20
KEY_VALUE_HEADS = 4
HEAD_SIZE = 128
DRAFT_TOKENS = 4

epsilon = 1e-05
LANES = 128
MIB = 2**20
F32 = jnp.float32
BF16 = jnp.bfloat16

IN_VMEM = pl.BlockSpec(memory_space=pltpu.VMEM)
IN_SMEM = pl.BlockSpec(memory_space=pltpu.SMEM)
ANYWHERE = pl.BlockSpec(memory_space=pl.ANY)


def round_up(n, m):
    return -(-n // m) * m


def silu(v):
    return v / (1.0 + jnp.exp(-v))


def dot_nt(a, b):
    return lax.dot_general(a, b, (((1,), (1,)), ((), ())), preferred_element_type=F32)


def dot_nn(a, b):
    return jnp.dot(a, b, preferred_element_type=F32)


def call(body, out_shape, args, specs, scratch=(), limit=16, flops=0, nbytes=0, name=None):
    outs = jax.tree.map(lambda _: IN_VMEM, out_shape)
    return pl.pallas_call(
        body,
        out_shape=out_shape,
        in_specs=specs,
        out_specs=outs,
        scratch_shapes=list(scratch),
        compiler_params=pltpu.CompilerParams(vmem_limit_bytes=limit * MIB),
        cost_estimate=pl.CostEstimate(flops=flops, bytes_accessed=nbytes, transcendentals=0),
        name=name,
    )(*args)


def project_body(order, place, x_ref, gain_ref, wm_ref, ws_ref, wt_ref, xg_ref, keep_ref, send_ref, xs):
    wide_at = place[0]
    mine = place[1]
    for i, rel in enumerate(order):
        xs[wide_at ^ rel] = x_ref[i].astype(F32)
    blocks, rows, width = xs.shape
    x = xs[...].reshape(blocks * rows, width)
    squares = jnp.sum(x * x, axis=1, keepdims=True)
    xg = (x * gain_ref[...]).astype(BF16)
    xg_ref[...] = xg
    columns = wm_ref.shape[1]
    padded = round_up(columns, LANES)
    shared = ws_ref.shape[0]
    shared_at = padded
    step_at = shared_at + round_up(shared, LANES)
    square_at = step_at + LANES
    heads = wt_ref.shape[1]
    both = dot_nt(xg, ws_ref[...])
    for ref, group in ((send_ref, 1 - mine), (keep_ref, mine)):
        ref[:, :columns] = dot_nt(xg, wm_ref[group])
        ref[:, shared_at : shared_at + shared] = both
        ref[:, step_at : step_at + heads] = dot_nt(xg, wt_ref[group])
        ref[:, square_at : square_at + LANES] = jnp.broadcast_to(squares, (blocks * rows, LANES))


def combine_body(width, heads, place, keep_ref, recv_ref, feat_ref, inv_ref, step_ref, ss):
    wide_at = place[0]
    blocks, rows, used = feat_ref.shape
    step_at = used
    square_at = step_at + LANES
    mean = (keep_ref[:, square_at:] + recv_ref[:, square_at:]) / width
    inv = lax.rsqrt(mean + epsilon)
    inv_ref[...] = inv
    feat = (keep_ref[:, :used] + recv_ref[:, :used]) * inv[:, :1]
    feat_ref[...] = feat.reshape(blocks, rows, used).astype(BF16)
    step = (keep_ref[:, step_at:square_at] + recv_ref[:, step_at:square_at]) * inv
    ss[...] = step.reshape(blocks, rows, LANES)
    step_ref[...] = ss[wide_at]


def mixer_body(
    dims,
    length_ref,
    feat_ref,
    step_ref,
    cos_ref,
    sin_ref,
    bias_ref,
    decay_ref,
    skip_ref,
    gain_ref,
    key_ref,
    value_ref,
    state_ref,
    out_ref,
    fs,
    bc,
    own,
):
    columns, shared, shared_at, q_heads, kv_heads, heads, head_width = dims
    t_count = DRAFT_TOKENS
    hs = HEAD_SIZE
    repeat = q_heads // kv_heads
    sources = feat_ref.shape[0]
    for i in range(sources):
        fs[:, i * columns : (i + 1) * columns] = feat_ref[i, :, :columns].astype(F32)
        bc[:, i * shared : (i + 1) * shared] = feat_ref[i, :, shared_at : shared_at + shared].astype(F32)
    length = length_ref[0]

    turned = q_heads + kv_heads
    stacked = jnp.concatenate([fs[:, h * hs : (h + 1) * hs] for h in range(turned)], axis=0)
    cos = jnp.concatenate([cos_ref[...]] * turned, axis=0)
    sin = jnp.concatenate([sin_ref[...]] * turned, axis=0)
    swapped = jnp.concatenate([stacked[:, hs // 2 :], stacked[:, : hs // 2]], axis=1)
    rotated = stacked * cos + swapped * sin
    slots = key_ref.shape[0]
    scale = hs ** (-0.5)
    group_rows = repeat * t_count
    live = lax.broadcasted_iota(jnp.int32, (group_rows, slots), 1) < length
    row_t = lax.broadcasted_iota(jnp.int32, (group_rows, LANES), 0) % t_count
    causal = lax.broadcasted_iota(jnp.int32, (group_rows, LANES), 1) <= row_t
    filler = jnp.zeros((LANES - t_count, hs), F32)
    for k in range(kv_heads):
        queries = rotated[k * group_rows : (k + 1) * group_rows].astype(BF16)
        at = q_heads * t_count + k * t_count
        new_keys = jnp.concatenate([rotated[at : at + t_count], filler], axis=0).astype(BF16)
        v_at = (turned + k) * hs
        new_values = jnp.concatenate([fs[:, v_at : v_at + hs], filler], axis=0).astype(BF16)
        head = slice(k * hs, (k + 1) * hs)
        cache = jnp.where(live, dot_nt(queries, key_ref[:, head]) * scale, -1e30)
        fresh = jnp.where(causal, dot_nt(queries, new_keys) * scale, -1e30)
        highest = jnp.maximum(
            jnp.max(cache, axis=1, keepdims=True), jnp.max(fresh, axis=1, keepdims=True)
        )
        cache = jnp.exp(cache - highest)
        fresh = jnp.exp(fresh - highest)
        total = jnp.sum(cache, axis=1, keepdims=True) + jnp.sum(fresh, axis=1, keepdims=True)
        attended = dot_nn((cache / total).astype(BF16), value_ref[:, head]) + dot_nn(
            (fresh / total).astype(BF16), new_values
        )
        for r in range(repeat):
            h = k * repeat + r
            own[:, h * hs : (h + 1) * hs] = attended[r * t_count : (r + 1) * t_count]

    x_at = (turned + kv_heads) * hs
    m_size = heads * head_width
    states = bc.shape[1] // 2
    x = silu(fs[:, x_at : x_at + m_size])
    gate = silu(fs[:, x_at + m_size : x_at + 2 * m_size])
    write = silu(bc[:, :states])
    read = silu(bc[:, states:])
    read_high = read.astype(BF16)
    read_low = (read - read_high.astype(F32)).astype(BF16)
    carried = dot_nt(read_high, state_ref[...]) + dot_nt(read_low, state_ref[...])
    raw = step_ref[:, :heads] + bias_ref[...]
    step = jnp.maximum(raw, 0.0) + jnp.log1p(jnp.exp(-jnp.abs(raw)))
    rate = -step * decay_ref[...]
    sums = [rate[0:1]]
    for t in range(1, t_count):
        sums.append(sums[-1] + rate[t : t + 1])
    sums = jnp.concatenate(sums, axis=0)

    def spread(v):
        return jnp.concatenate(
            [jnp.broadcast_to(v[:, h : h + 1], (v.shape[0], head_width)) for h in range(heads)], axis=1
        )

    sums = spread(sums)
    pushed = spread(step) * x
    skip = spread(skip_ref[...])
    readout = []
    for t in range(t_count):
        row = jnp.exp(sums[t : t + 1]) * carried[t : t + 1] + skip * x[t : t + 1]
        for s in range(t + 1):
            overlap = jnp.sum(write[s : s + 1] * read[t : t + 1], axis=1, keepdims=True)
            term = pushed[s : s + 1] * overlap
            if s < t:
                term = term * jnp.exp(sums[t : t + 1] - sums[s : s + 1])
            row = row + term
        readout.append(row)
    gated = jnp.concatenate(readout, axis=0) * gate
    tall = jnp.concatenate([gated[:, h * head_width : (h + 1) * head_width] for h in range(heads)], axis=0)
    tall = tall * lax.rsqrt(jnp.mean(tall * tall, axis=1, keepdims=True) + epsilon)
    m_at = q_heads * hs
    for h in range(heads):
        a = h * head_width
        own[:, m_at + a : m_at + a + head_width] = (
            tall[h * t_count : (h + 1) * t_count] * gain_ref[:, a : a + head_width]
        )
    targets, _, piece = out_ref.shape
    for i in range(targets):
        out_ref[i] = own[:, i * piece : (i + 1) * piece].astype(BF16)


def gate_up_body(xg_ref, inv_ref, gate_ref, up_ref, own_ref, send_ref):
    rows, columns = xg_ref.shape[0], gate_ref.shape[1]
    xg = xg_ref[...]
    inv = inv_ref[:, :1]
    half = own_ref.shape[1] // 2
    for w_ref, at in ((gate_ref, 0), (up_ref, half)):
        part = dot_nn(xg, w_ref[...]) * inv
        own_ref[:, at : at + columns] = part
        send_ref[:, at : at + columns] = part.astype(BF16)


def down_body(own_ref, recv_ref, down_ref, after_ref, out_ref):
    columns = down_ref.shape[0]
    half = own_ref.shape[1] // 2
    gate = own_ref[:, :columns] + recv_ref[:, :columns].astype(F32)
    up = own_ref[:, half : half + columns] + recv_ref[:, half : half + columns].astype(F32)
    hidden = (silu(gate) * up).astype(BF16)
    out_ref[...] = dot_nn(hidden, down_ref[...])


def output_body(place, mine_ref, other_ref, w_ref, ff_ref, out_ref):
    me = place[1]
    blocks, rows, piece = mine_ref.shape
    a = mine_ref[...].astype(F32).reshape(blocks * rows, piece).astype(BF16)
    b = other_ref[...].astype(F32).reshape(blocks * rows, piece).astype(BF16)
    total = ff_ref[...] + dot_nn(a, w_ref[me]) + dot_nn(b, w_ref[1 - me])
    out_ref[...] = total.reshape(blocks, rows, total.shape[1]).astype(BF16)


def on_device(
    tokens,
    norm_gain,
    mixer_in,
    shared_in,
    step_in,
    step_bias,
    decay_rate,
    skip_gain,
    cached_keys,
    cached_values,
    lengths,
    state_cache,
    mixer_gain,
    mixer_out,
    gate_weight,
    up_weight,
    down_weight,
):
    n_short = lax.axis_size("short")
    n_wide = lax.axis_size("wide")
    own_rows, width = tokens.shape
    rows = own_rows * n_wide
    columns = mixer_in.shape[2]
    shared = shared_in.shape[1]
    heads = step_bias.shape[0]
    head_width = state_cache.shape[2]
    states = state_cache.shape[3]
    q_heads = QUERY_HEADS // n_short
    kv_heads = KEY_VALUE_HEADS // n_short
    slots = cached_keys.shape[1]
    ff = gate_weight.shape[1]
    piece = mixer_out.shape[1]
    place = jnp.stack([lax.axis_index("wide"), lax.axis_index("short")]).astype(jnp.int32)
    other_core = [(0, 1), (1, 0)]

    gathered = tokens[None]
    order = [0]
    stride = n_wide // 2
    while stride:
        moved = lax.ppermute(gathered, "wide", [(j, j ^ stride) for j in range(n_wide)])
        gathered = jnp.concatenate([gathered, moved], axis=0)
        order = order + [rel ^ stride for rel in order]
        stride //= 2

    used = round_up(columns, LANES) + round_up(shared, LANES)
    sent = used + 2 * LANES
    wm = jnp.transpose(mixer_in, (1, 2, 0))
    ws = jnp.transpose(shared_in)
    wt = jnp.transpose(step_in).reshape(n_short, heads, width)
    weights = (wm.size + ws.size + wt.size) * 2
    xg, keep, send = call(
        functools.partial(project_body, order),
        (
            jax.ShapeDtypeStruct((rows, width), BF16),
            jax.ShapeDtypeStruct((rows, sent), F32),
            jax.ShapeDtypeStruct((rows, sent), F32),
        ),
        (place, gathered, norm_gain.reshape(1, width), wm, ws, wt),
        [IN_SMEM] + [IN_VMEM] * 5,
        [pltpu.VMEM((n_wide, own_rows, width), F32)],
        flops=rows * weights,
        nbytes=weights,
        name="project",
    )
    received = lax.ppermute(send, "short", other_core)
    features, inv, step_raw = call(
        functools.partial(combine_body, width * n_short, heads),
        (
            jax.ShapeDtypeStruct((n_wide, own_rows, used), BF16),
            jax.ShapeDtypeStruct((rows, LANES), F32),
            jax.ShapeDtypeStruct((own_rows, LANES), F32),
        ),
        (place, keep, received),
        [IN_SMEM, IN_VMEM, IN_VMEM],
        [pltpu.VMEM((n_wide, own_rows, LANES), F32)],
        flops=4 * rows * sent,
        nbytes=8 * rows * sent,
        name="combine",
    )
    features = lax.all_to_all(features, "wide", split_axis=0, concat_axis=0, tiled=True)

    half = round_up(ff, LANES)
    ff_own, ff_send = call(
        gate_up_body,
        (
            jax.ShapeDtypeStruct((rows, 2 * half), F32),
            jax.ShapeDtypeStruct((rows, 2 * half), BF16),
        ),
        (xg, inv, gate_weight, up_weight),
        [IN_VMEM] * 4,
        flops=4 * rows * width * ff,
        nbytes=4 * width * ff,
        name="gate_up",
    )
    ff_received = lax.ppermute(ff_send, "short", other_core)

    half_head = HEAD_SIZE // 2
    frequency = 10000.0 ** (-(jnp.arange(half_head, dtype=F32) * 2.0 / HEAD_SIZE))
    positions = lengths[0] + jnp.arange(own_rows, dtype=jnp.int32)
    angles = positions.astype(F32)[:, None] * frequency
    cos = jnp.cos(angles)
    sin = jnp.sin(angles)
    cos = jnp.concatenate([cos, cos], axis=1)
    sin = jnp.concatenate([-sin, sin], axis=1)
    mixed_rows = call(
        functools.partial(
            mixer_body,
            (columns, shared, round_up(columns, LANES), q_heads, kv_heads, heads, head_width),
        ),
        jax.ShapeDtypeStruct((n_wide, own_rows, piece), BF16),
        (
            lengths,
            features,
            step_raw,
            cos,
            sin,
            step_bias.reshape(1, heads),
            decay_rate.reshape(1, heads),
            skip_gain.reshape(1, heads),
            mixer_gain.reshape(1, heads * head_width),
            cached_keys[0],
            cached_values[0],
            state_cache.reshape(heads * head_width, states),
        ),
        [IN_SMEM] + [IN_VMEM] * 11,
        [
            pltpu.VMEM((own_rows, n_wide * columns), F32),
            pltpu.VMEM((own_rows, n_wide * shared), F32),
            pltpu.VMEM((own_rows, n_wide * piece), F32),
        ],
        flops=4 * own_rows * state_cache.size,
        nbytes=6 * state_cache.size,
        name="mixers",
    )
    returned = lax.all_to_all(mixed_rows, "wide", split_axis=0, concat_axis=0, tiled=True)
    other = lax.ppermute(returned, "short", other_core)
    ff_out = call(
        down_body,
        jax.ShapeDtypeStruct((rows, width), F32),
        (ff_own, ff_received, down_weight, mixed_rows),
        [IN_VMEM] * 3 + [ANYWHERE],
        flops=2 * rows * width * ff,
        nbytes=2 * width * ff,
        name="down",
    )
    summed = call(
        output_body,
        jax.ShapeDtypeStruct((n_wide, own_rows, width), BF16),
        (place, returned, other, mixer_out, ff_out),
        [IN_SMEM] + [IN_VMEM] * 4,
        flops=4 * rows * width * piece,
        nbytes=4 * width * piece,
        name="output",
    )
    pieces = lax.all_to_all(summed, "wide", split_axis=0, concat_axis=0, tiled=True)
    total = tokens.astype(F32) + jnp.sum(pieces.astype(F32), axis=0)
    return total.astype(BF16)


def solution(mesh):
    in_specs = (
        P(("groups", "wide"), "short"),
        P("short"),
        P("short", None, "wide"),
        P("short", "wide"),
        P("short", None),
        P("short"),
        P("short"),
        P("short"),
        P(("groups", "wide"), None, "short"),
        P(("groups", "wide"), None, "short"),
        P(("groups", "wide")),
        P(("groups", "wide"), "short", None, None),
        P("short"),
        P(None, "wide", "short"),
        P("short", "wide"),
        P("short", "wide"),
        P("wide", "short"),
    )
    out_specs = P(("groups", "wide"), "short")
    return jax.shard_map(
        on_device, mesh=mesh, in_specs=in_specs, out_specs=out_specs, check_vma=False
    )
```

time: 177 us -> 87.5 us (0.49)
  matrix products: 45.4 us -> 0 us
  blocking collectives: 53.5 us -> 19.9 us
  other arithmetic: 24.1 us -> 3.37 us
  Pallas kernels: 0 us -> 14.4 us
  between operations: 14.2 us -> 0.83 us
  local copies, waits for them, and re-layouts: 13.2 us -> 20.5 us
  waiting for transfers between devices: 10.4 us -> 13.3 us
    dot_general x14 -> x0, matrix products: 43.6 us -> none  [the longest x4 10.6 us: scan_one(): jnp.einsum('hpn,n->hp', hstate, read_vec[draft_index], precision=lax.Prec...]
    all_gather x3 -> x0, blocking collectives: 36.2 us -> none  [the longest x1 32.2 us: on_device(): gathered = lax.all_gather(normed, 'wide', axis=0, tiled=True)]
    unnamed x3 -> x1, other arithmetic: 19.2 us -> 0.01 us
    pallas_call x0 -> x6, Pallas kernels: none -> 14.4 us  [call(): pl.pallas_call(body, out_shape=out_shape, in_specs=specs, out_specs=outs,...]
    unnamed x30 -> x32, local copies, waits for them, and re-layouts: 6.24 us -> 19.8 us
    all_to_all x1 -> x2, blocking collectives: 10.5 us -> 19.9 us  [the longest x1 10.8 us: on_device(): lax.all_to_all(summed, 'wide', split_axis=0, concat_axis=0, tiled=True)]
    all_to_all x3 -> x1, starting transfers between devices: 14.9 us -> 6.26 us  [on_device(): lax.all_to_all(features, 'wide', split_axis=0, concat_axis=0, tiled=True)]
    ppermute x0 -> x6, starting transfers between devices: none -> 8.22 us  [the longest x3 7.98 us: on_device(): lax.ppermute(gathered, 'wide', [(j, j ^ stride) for j in range(n_wide)])]
  transfers between devices with their start and end apart: 6 -> 7, of which waited for: 2 -> 5; matrix products, arithmetic and copies ran while one was open for 36% -> 1% of each run, Pallas kernels for 0% -> 5%
where the time goes in v1:
time: 87.5 us; the launch traced here: 86.8 us
  local copies, waits for them, and re-layouts  20.5 us (23%)
  blocking collectives  19.9 us (23%)
  starting transfers between devices  14.5 us (17%)
  Pallas kernels  14.4 us (16%)
  waiting for transfers between devices  13.3 us (15%)
  other arithmetic  3.37 us (4%)
    unnamed x32, local copies, waits for them, and re-layouts  19.8 us
    pallas_call x6, Pallas kernels, call(): pl.pallas_call(body, out_shape=out_shape, in_specs=specs, out_specs=outs,...  14.4 us
    all_to_all x1, blocking collectives, on_device(): lax.all_to_all(summed, 'wide', split_axis=0, concat_axis=0, tiled=True)  10.8 us
    all_to_all x1, blocking collectives, on_device(): lax.all_to_all(mixed_rows, 'wide', split_axis=0, concat_axis=0, tiled=True)  9.06 us
    ppermute x3, starting transfers between devices, on_device(): lax.ppermute(gathered, 'wide', [(j, j ^ stride) for j in range(n_wide)])  7.98 us
    all_to_all x1, waiting for transfers between devices, on_device(): lax.all_to_all(features, 'wide', split_axis=0, concat_axis=0, tiled=True)  6.77 us
    all_to_all x1, starting transfers between devices, on_device(): lax.all_to_all(features, 'wide', split_axis=0, concat_axis=0, tiled=True)  6.26 us
    ppermute x3, waiting for transfers between devices, on_device(): lax.ppermute(gathered, 'wide', [(j, j ^ stride) for j in range(n_wide)])  5.82 us
  transfers between devices with their start and end apart: 7, of which 5 were waited for; matrix products, arithmetic and copies ran while one was open for 1% of the time, Pallas kernels for 5%

profile of v1, /device:TPU:0, one launch (start us, length us, event | category | flops | bytes accessed | tf_op | source)
XLA Modules:
  0.0 86.8 jit_solution(888735726959523077)
XLA Ops:
  0.0 4.0 %collective-permute-start = (bf16[1,4,2560]{2,1,0:T(4,128)(2,1)}, bf16[1,4,2560]{2,1,0:T(4,128)(2,1)S(1)}, u32[]{:S(2)}, u32[]{:S(2)}) collective-permute-start(bf16[1,4,2560]{2,1,0:T(4,128)(2,1)} %bitcast.29), channel_id=1, source_target_pairs={{0,8},{2,10},{4,12},{6,14},{8,0},{10,2},{12,4},{14,6},{1,9},{3,11}... | collective-permute-start | bytes 61448 | tf_op jit(solution)/shard_map/ppermute | solution.py:279
  4.0 2.0 %collective-permute-done = bf16[1,4,2560]{2,1,0:T(4,128)(2,1)S(1)} collective-permute-done((bf16[1,4,2560]{2,1,0:T(4,128)(2,1)}, bf16[1,4,2560]{2,1,0:T(4,128)(2,1)S(1)}, u32[]{:S(2)}, u32[]{:S(2)}) %collective-permute-start) | collective-permute-done | bytes 20512 | tf_op jit(solution)/shard_map/ppermute | solution.py:279
  6.8 2.0 %collective-permute-start.1 = (bf16[2,4,2560]{2,1,0:T(4,128)(2,1)S(1)}, bf16[2,4,2560]{2,1,0:T(4,128)(2,1)S(1)}, u32[]{:S(2)}, u32[]{:S(2)}) collective-permute-start(bf16[2,4,2560]{2,1,0:T(4,128)(2,1)S(1)} %pad_maximum_fusion.2), channel_id=1, source_target_pairs={{0,4},{2,6},{4,0},{6,2},{8,12},{10,14},{12,8},{14,10},{1,5},{3,7},... | collective-permute-start | bytes 122888 | tf_op jit(solution)/shard_map/ppermute | solution.py:279
  9.5 1.4 %collective-permute-done.1 = bf16[2,4,2560]{2,1,0:T(4,128)(2,1)S(1)} collective-permute-done((bf16[2,4,2560]{2,1,0:T(4,128)(2,1)S(1)}, bf16[2,4,2560]{2,1,0:T(4,128)(2,1)S(1)}, u32[]{:S(2)}, u32[]{:S(2)}) %collective-permute-start.1) | collective-permute-done | bytes 40992 | tf_op jit(solution)/shard_map/ppermute | solution.py:279
  10.8 0.8 pad_maximum_fusion.1
  11.6 2.0 %collective-permute-start.2 = (bf16[4,4,2560]{2,1,0:T(4,128)(2,1)S(1)}, bf16[4,4,2560]{2,1,0:T(4,128)(2,1)S(1)}, u32[]{:S(2)}, u32[]{:S(2)}) collective-permute-start(bf16[4,4,2560]{2,1,0:T(4,128)(2,1)S(1)} %pad_maximum_fusion.1), channel_id=1, source_target_pairs={{0,2},{2,0},{4,6},{6,4},{8,10},{10,8},{12,14},{14,12},{1,3},{3,1},... | collective-permute-start | bytes 245768 | tf_op jit(solution)/shard_map/ppermute | solution.py:279
  13.7 2.5 %collective-permute-done.2 = bf16[4,4,2560]{2,1,0:T(4,128)(2,1)S(1)} collective-permute-done((bf16[4,4,2560]{2,1,0:T(4,128)(2,1)S(1)}, bf16[4,4,2560]{2,1,0:T(4,128)(2,1)S(1)}, u32[]{:S(2)}, u32[]{:S(2)}) %collective-permute-start.2) | collective-permute-done | bytes 81952 | tf_op jit(solution)/shard_map/ppermute | solution.py:279
  16.1 0.8 pad_maximum_fusion.x_ref
  17.0 3.1 %copy-done.3 = bf16[2560,2,736]{0,2,1:T(8,128)(2,1)S(1)} copy-done((bf16[2560,2,736]{0,2,1:T(8,128)(2,1)S(1)}, bf16[2560,2,736]{0,2,1:T(8,128)(2,1)}, u32[]{:S(2)}) %copy-start.3) | copy-done | bytes 7536664
  20.1 1.0 %copy-done.5 = bf16[2560,64]{0,1:T(8,128)(2,1)S(1)} copy-done((bf16[2560,64]{0,1:T(8,128)(2,1)S(1)}, bf16[2560,64]{0,1:T(8,128)(2,1)}, u32[]{:S(2)}) %copy-start.5) | copy-done | bytes 327704
  21.1 0.9 %copy-done.8 = bf16[2560,32]{0,1:T(8,128)(2,1)S(1)} copy-done((bf16[2560,32]{0,1:T(8,128)(2,1)S(1)}, bf16[2560,32]{0,1:T(8,128)(2,1)}, u32[]{:S(2)}) %copy-start.8) | copy-done | bytes 163864
  22.0 2.9 %project.1 = (bf16[32,2560]{1,0:T(8,128)(2,1)S(1)}, f32[32,1152]{1,0:T(8,128)S(1)}, f32[32,1152]{1,0:T(8,128)S(1)}) custom-call(s32[2]{0:T(128)S(1)} %pad_add_fusion.place, bf16[8,4,2560]{2,1,0:T(4,128)(2,1)S(1)} %pad_maximum_fusion.x_ref, f32[1,2560]{1,0:T(1,128)S(1)} %reshape.32.gain_ref, bf16[2,736,2560]{2,1,0:T(8,128)(2,1)S(1)} %bitcast.17, ...), custom_call_target="tpu_custom_call" | custom-call | flops 256901120 | bytes 8028160 | tf_op jit(solution)/shard_map/project/pallas_call | solution.py:44
  26.3 1.3 %combine.1 = (bf16[8,4,896]{2,1,0:T(4,128)(2,1)}, f32[32,128]{1,0:T(8,128)S(1)}, f32[4,128]{1,0:T(4,128)S(1)}) custom-call(s32[2]{0:T(128)S(1)} %pad_add_fusion.place, f32[32,1152]{1,0:T(8,128)S(1)} %get-tuple-element.13.keep_ref, f32[32,1152]{1,0:T(8,128)S(1)} %collective-permute-done.3.recv_ref), custom_call_target="tpu_custom_call" | custom-call | flops 147456 | bytes 294912 | tf_op jit(solution)/shard_map/combine/pallas_call | solution.py:44
  27.6 4.9 %copy-done = bf16[2560,2688]{1,0:T(8,128)(2,1)S(1)} copy-done((bf16[2560,2688]{1,0:T(8,128)(2,1)S(1)}, bf16[2560,2688]{1,0:T(8,128)(2,1)}, u32[]{:S(2)}) %copy-start) | copy-done | bytes 13762584
  32.5 4.9 %copy-done.1 = bf16[2560,2688]{1,0:T(8,128)(2,1)S(1)} copy-done((bf16[2560,2688]{1,0:T(8,128)(2,1)S(1)}, bf16[2560,2688]{1,0:T(8,128)(2,1)}, u32[]{:S(2)}) %copy-start.1) | copy-done | bytes 13762584
  37.4 4.8 %gate_up.1 = (f32[32,5376]{1,0:T(8,128)S(1)}, bf16[32,5376]{1,0:T(8,128)(2,1)S(1)}) custom-call(bf16[32,2560]{1,0:T(8,128)(2,1)S(1)} %get-tuple-element.17.xg_ref, f32[32,128]{1,0:T(8,128)S(1)} %get-tuple-element.18.inv_ref, bf16[2560,2688]{1,0:T(8,128)(2,1)S(1)} %copy-done, bf16[2560,2688]{1,0:T(8,128)(2,1)S(1)} %copy-done.1), custom_call_target="tpu_custom_call" | custom-call | flops 880803840 | bytes 27525120 | tf_op jit(solution)/shard_map/gate_up/pallas_call | solution.py:44
  42.6 6.3 %all-to-all-start = ((bf16[8,4,896]{2,1,0:T(4,128)(2,1)}), bf16[8,4,896]{2,1,0:T(4,128)(2,1)S(1)}, u32[]{:S(2)}, u32[]{:S(2)}) async-start(bf16[8,4,896]{2,1,0:T(4,128)(2,1)} %get-tuple-element.15), calls=%async_computation | async-start | bytes 114688 | tf_op jit(solution)/shard_map/all_to_all | solution.py:319
  48.9 6.8 %all-to-all-done.feat_ref = bf16[8,4,896]{2,1,0:T(4,128)(2,1)S(1)} async-done(((bf16[8,4,896]{2,1,0:T(4,128)(2,1)}), bf16[8,4,896]{2,1,0:T(4,128)(2,1)S(1)}, u32[]{:S(2)}, u32[]{:S(2)}) %all-to-all-start) | async-done | bytes 57376 | tf_op jit(solution)/shard_map/all_to_all | solution.py:319
  55.7 1.7 %mixers.1.after_ref = bf16[8,4,416]{2,1,0:T(4,128)(2,1)S(1)} custom-call(s32[1]{0:T(128)} %copy.18.length_ref, bf16[8,4,896]{2,1,0:T(4,128)(2,1)S(1)} %all-to-all-done.feat_ref, f32[4,128]{1,0:T(4,128)S(1)} %get-tuple-element.16.step_ref, f32[4,128]{1,0:T(4,128)S(1)} %get-tuple-element.24.cos_ref, f32[4,128]{1,0:T(4,128)S(1)} %get-tuple-element.25.sin_ref, ...), custom_call_target="tpu_custom_call" | custom-call | flops 8388608 | bytes 3145728 | tf_op jit(solution)/shard_map/mixers/pallas_call | solution.py:44
  57.4 9.1 %all_to_all.15.mine_ref = bf16[8,4,416]{2,1,0:T(4,128)(2,1)S(1)} all-to-all(bf16[8,4,416]{2,1,0:T(4,128)(2,1)S(1)} %mixers.1.after_ref), channel_id=1, replica_groups=mesh['groups'=2,'wide'=8,'short'=2] {'wide'}, dimensions={0} | all-to-all | bytes 53248 | tf_op jit(solution)/shard_map/all_to_all | solution.py:374
  66.5 4.9 %copy-done.2 = bf16[2688,2560]{1,0:T(8,128)(2,1)S(1)} copy-done((bf16[2688,2560]{1,0:T(8,128)(2,1)S(1)}, bf16[2688,2560]{1,0:T(8,128)(2,1)}, u32[]{:S(2)}) %copy-start.2) | copy-done | bytes 13762584
  71.4 2.4 %down.1.ff_ref = f32[32,2560]{1,0:T(8,128)S(1)} custom-call(f32[32,5376]{1,0:T(8,128)S(1)} %get-tuple-element.19.own_ref, bf16[32,5376]{1,0:T(8,128)(2,1)S(1)} %collective-permute-done.5.recv_ref, bf16[2688,2560]{1,0:T(8,128)(2,1)S(1)} %copy-done.2, bf16[8,4,416]{2,1,0:T(4,128)(2,1)S(1)} %mixers.1.after_ref), custom_call_target="tpu_custom_call" | custom-call | flops 440401920 | bytes 13762560 | tf_op jit(solution)/shard_map/down/pallas_call | solution.py:44
  73.8 1.4 %output.1 = bf16[8,4,2560]{2,1,0:T(4,128)(2,1)S(1)} custom-call(s32[2]{0:T(128)S(1)} %pad_add_fusion.place, bf16[8,4,416]{2,1,0:T(4,128)(2,1)S(1)} %all_to_all.15.mine_ref, bf16[8,4,416]{2,1,0:T(4,128)(2,1)S(1)} %collective-permute-done.4.other_ref, bf16[2,416,2560]{2,1,0:T(8,128)(2,1)S(1)} %bitcast.19, f32[32,2560]{1,0:T(8,128)S(1)} %down.1.ff_ref), custom_call_target="tpu_custom_call" | custom-call | flops 136314880 | bytes 4259840 | tf_op jit(solution)/shard_map/output/pallas_call | solution.py:44
  75.3 10.8 %all_to_all.16 = bf16[8,4,2560]{2,1,0:T(4,128)(2,1)S(1)} all-to-all(bf16[8,4,2560]{2,1,0:T(4,128)(2,1)S(1)} %output.1), channel_id=1, replica_groups=mesh['groups'=2,'wide'=8,'short'=2] {'wide'}, dimensions={0} | all-to-all | bytes 327680 | tf_op jit(solution)/shard_map/all_to_all | solution.py:394
  (42 shorter events, 3.5 us)
Async XLA Ops:
  0.0 6.0 %collective-permute-start = (bf16[1,4,2560]{2,1,0:T(4,128)(2,1)}, bf16[1,4,2560]{2,1,0:T(4,128)(2,1)S(1)}, u32[]{:S(2)}, u32[]{:S(2)}) collective-permute-start(bf16[1,4,2560]{2,1,0:T(4,128)(2,1)} %bitcast.29), channel_id=1, source_target_pairs={{0,8},{2,10},{4,12},{6,14},{8,0},{10,2},{12,4},{14,6},{1,9},{3,11}... | collective-permute-start | bytes 61448 | tf_op jit(solution)/shard_map/ppermute | solution.py:279
  6.8 4.1 %collective-permute-start.1 = (bf16[2,4,2560]{2,1,0:T(4,128)(2,1)S(1)}, bf16[2,4,2560]{2,1,0:T(4,128)(2,1)S(1)}, u32[]{:S(2)}, u32[]{:S(2)}) collective-permute-start(bf16[2,4,2560]{2,1,0:T(4,128)(2,1)S(1)} %pad_maximum_fusion.2), channel_id=1, source_target_pairs={{0,4},{2,6},{4,0},{6,2},{8,12},{10,14},{12,8},{14,10},{1,5},{3,7},... | collective-permute-start | bytes 122888 | tf_op jit(solution)/shard_map/ppermute | solution.py:279
  11.6 4.5 %collective-permute-start.2 = (bf16[4,4,2560]{2,1,0:T(4,128)(2,1)S(1)}, bf16[4,4,2560]{2,1,0:T(4,128)(2,1)S(1)}, u32[]{:S(2)}, u32[]{:S(2)}) collective-permute-start(bf16[4,4,2560]{2,1,0:T(4,128)(2,1)S(1)} %pad_maximum_fusion.1), channel_id=1, source_target_pairs={{0,2},{2,0},{4,6},{6,4},{8,10},{10,8},{12,14},{14,12},{1,3},{3,1},... | collective-permute-start | bytes 245768 | tf_op jit(solution)/shard_map/ppermute | solution.py:279
  17.0 3.1 %copy-start.3 = (bf16[2560,2,736]{0,2,1:T(8,128)(2,1)S(1)}, bf16[2560,2,736]{0,2,1:T(8,128)(2,1)}, u32[]{:S(2)}) copy-start(bf16[2560,2,736]{0,2,1:T(8,128)(2,1)} %param.19) | copy-start | bytes 22609924
  20.1 1.0 %copy-start.5 = (bf16[2560,64]{0,1:T(8,128)(2,1)S(1)}, bf16[2560,64]{0,1:T(8,128)(2,1)}, u32[]{:S(2)}) copy-start(bf16[2560,64]{0,1:T(8,128)(2,1)} %param.20) | copy-start | bytes 983044
  21.1 0.9 %copy-start.8 = (bf16[2560,32]{0,1:T(8,128)(2,1)S(1)}, bf16[2560,32]{0,1:T(8,128)(2,1)}, u32[]{:S(2)}) copy-start(bf16[2560,32]{0,1:T(8,128)(2,1)} %param.21) | copy-start | bytes 491524
  24.9 1.4 %collective-permute-start.3 = (f32[32,1152]{1,0:T(8,128)S(1)}, f32[32,1152]{1,0:T(8,128)S(1)}, u32[]{:S(2)}, u32[]{:S(2)}) collective-permute-start(f32[32,1152]{1,0:T(8,128)S(1)} %get-tuple-element.14), channel_id=1, source_target_pairs={{0,1},{1,0},{2,3},{3,2},{4,5},{5,4},{6,7},{7,6},{8,9},{9,8},{10,11... | collective-permute-start | bytes 442376 | tf_op jit(solution)/shard_map/ppermute | solution.py:304
  27.6 4.9 %copy-start = (bf16[2560,2688]{1,0:T(8,128)(2,1)S(1)}, bf16[2560,2688]{1,0:T(8,128)(2,1)}, u32[]{:S(2)}) copy-start(bf16[2560,2688]{1,0:T(8,128)(2,1)} %gate_ref.1) | copy-start | bytes 41287684
  32.5 4.9 %copy-start.1 = (bf16[2560,2688]{1,0:T(8,128)(2,1)S(1)}, bf16[2560,2688]{1,0:T(8,128)(2,1)}, u32[]{:S(2)}) copy-start(bf16[2560,2688]{1,0:T(8,128)(2,1)} %up_ref.1) | copy-start | bytes 41287684
  37.4 18.3 %copy-start.4 = (bf16[1,16,128,256]{3,2,1,0:T(8,128)(2,1)S(1)}, bf16[1,16,128,256]{3,2,1,0:T(8,128)(2,1)}, u32[]{:S(2)}) copy-start(bf16[1,16,128,256]{3,2,1,0:T(8,128)(2,1)} %param.28) | copy-start | bytes 3145732
  37.4 18.3 %copy-start.6 = (bf16[1,512,256]{2,1,0:T(8,128)(2,1)S(1)}, bf16[1,512,256]{2,1,0:T(8,128)(2,1)}, u32[]{:S(2)}) copy-start(bf16[1,512,256]{2,1,0:T(8,128)(2,1)} %param.25) | copy-start | bytes 786436
  37.4 18.3 %copy-start.7 = (bf16[1,512,256]{2,1,0:T(8,128)(2,1)S(1)}, bf16[1,512,256]{2,1,0:T(8,128)(2,1)}, u32[]{:S(2)}) copy-start(bf16[1,512,256]{2,1,0:T(8,128)(2,1)} %param.26) | copy-start | bytes 786436
  37.4 18.3 %copy-start.9 = (f32[2048]{0:T(1024)S(1)}, f32[2048]{0:T(1024)}, u32[]{:S(2)}) copy-start(f32[2048]{0:T(1024)} %param.29) | copy-start | bytes 24580
  37.4 18.3 %copy-start.10 = (f32[16]{0:T(128)S(1)}, f32[16]{0:T(128)}, u32[]{:S(2)}) copy-start(f32[16]{0:T(128)} %param.22) | copy-start | bytes 196
  37.4 18.3 %copy-start.11 = (f32[16]{0:T(128)S(1)}, f32[16]{0:T(128)}, u32[]{:S(2)}) copy-start(f32[16]{0:T(128)} %param.23) | copy-start | bytes 196
  37.4 18.3 %copy-start.12 = (f32[16]{0:T(128)S(1)}, f32[16]{0:T(128)}, u32[]{:S(2)}) copy-start(f32[16]{0:T(128)} %param.24) | copy-start | bytes 196
  42.2 31.6 %slice-start = ((s8[4259840]{0:T(1024)(128)(4,1)}), s8[65536]{0:T(1024)(128)(4,1)S(1)}, s32[]{:S(2)}) async-start(s8[4259840]{0:T(1024)(128)(4,1)} %bitcast.18), calls=%async_computation.3 | async-start | bytes 131072
  42.2 43.9 %copy-start.13 = (bf16[4,2560]{1,0:T(4,128)(2,1)S(1)}, bf16[4,2560]{1,0:T(4,128)(2,1)}, u32[]{:S(2)}) copy-start(bf16[4,2560]{1,0:T(4,128)(2,1)} %param.17) | copy-start | bytes 61444
  42.2 24.2 %collective-permute-start.5 = (bf16[32,5376]{1,0:T(8,128)(2,1)S(1)}, bf16[32,5376]{1,0:T(8,128)(2,1)S(1)}, u32[]{:S(2)}, u32[]{:S(2)}) collective-permute-start(bf16[32,5376]{1,0:T(8,128)(2,1)S(1)} %get-tuple-element.20), channel_id=1, source_target_pairs={{0,1},{1,0},{2,3},{3,2},{4,5},{5,4},{6,7},{7,6},{8,9},{9,8},{10,11... | collective-permute-start | bytes 1032200 | tf_op jit(solution)/shard_map/ppermute | solution.py:334
  42.6 13.1 %all-to-all-start = ((bf16[8,4,896]{2,1,0:T(4,128)(2,1)}), bf16[8,4,896]{2,1,0:T(4,128)(2,1)S(1)}, u32[]{:S(2)}, u32[]{:S(2)}) async-start(bf16[8,4,896]{2,1,0:T(4,128)(2,1)} %get-tuple-element.15), calls=%async_computation | async-start | bytes 114688 | tf_op jit(solution)/shard_map/all_to_all | solution.py:319
  66.5 7.3 %collective-permute-start.4 = (bf16[8,4,416]{2,1,0:T(4,128)(2,1)S(1)}, bf16[8,4,416]{2,1,0:T(4,128)(2,1)S(1)}, u32[]{:S(2)}, u32[]{:S(2)}) collective-permute-start(bf16[8,4,416]{2,1,0:T(4,128)(2,1)S(1)} %all_to_all.15.mine_ref), channel_id=1, source_target_pairs={{0,1},{1,0},{2,3},{3,2},{4,5},{5,4},{6,7},{7,6},{8,9},{9,8},{10,11... | collective-permute-start | bytes 79880 | tf_op jit(solution)/shard_map/ppermute | solution.py:375
  66.5 4.9 %copy-start.2 = (bf16[2688,2560]{1,0:T(8,128)(2,1)S(1)}, bf16[2688,2560]{1,0:T(8,128)(2,1)}, u32[]{:S(2)}) copy-start(bf16[2688,2560]{1,0:T(8,128)(2,1)} %down_ref.1) | copy-start | bytes 41287684
  71.4 2.4 %slice-start.1 = ((s8[4259840]{0:T(1024)(128)(4,1)}), s8[4194304]{0:T(1024)(128)(4,1)S(1)}, s32[]{:S(2)}) async-start(s8[4259840]{0:T(1024)(128)(4,1)} %bitcast.18), calls=%async_computation.4 | async-start | bytes 8388608

commit v2 on v1

v2 whole, which is shorter than its diff:
```python
import functools

import jax
import jax.numpy as jnp
from jax import lax
from jax.experimental import pallas as pl
from jax.experimental.pallas import tpu as pltpu
from jax.sharding import PartitionSpec as P

QUERY_HEADS = 20
KEY_VALUE_HEADS = 4
HEAD_SIZE = 128
DRAFT_TOKENS = 4

epsilon = 1e-05
LANES = 128
BLOCK_COLUMNS = 384
BLOCK_DEPTH = 256
F32 = jnp.float32
BF16 = jnp.bfloat16

IN_VMEM = pl.BlockSpec(memory_space=pltpu.VMEM)
IN_SMEM = pl.BlockSpec(memory_space=pltpu.SMEM)
ANYWHERE = pl.BlockSpec(memory_space=pl.ANY)


def round_up(n, m):
    return -(-n // m) * m


def silu(v):
    return v / (1.0 + jnp.exp(-v))


def dot_nt(a, b):
    return lax.dot_general(a, b, (((1,), (1,)), ((), ())), preferred_element_type=F32)


def dot_nn(a, b):
    return jnp.dot(a, b, preferred_element_type=F32)


def kernel_room():
    n_wide = lax.axis_size("wide")
    return min(max(6 * n_wide // 8, 6), 48) * 2**20


def blocked_dot(x_ref, w_ref, done):
    depth, columns = w_ref.shape
    for at in range(0, columns, BLOCK_COLUMNS):
        here = slice(at, min(at + BLOCK_COLUMNS, columns))
        sums = None
        for k in range(0, depth, BLOCK_DEPTH):
            along = slice(k, min(k + BLOCK_DEPTH, depth))
            part = dot_nn(x_ref[:, along], w_ref[along, here])
            sums = part if sums is None else sums + part
        done(here, sums)


def call(body, out_shape, args, specs, scratch=(), flops=0, nbytes=0, name=None):
    outs = jax.tree.map(lambda _: IN_VMEM, out_shape)
    return pl.pallas_call(
        body,
        out_shape=out_shape,
        in_specs=specs,
        out_specs=outs,
        scratch_shapes=list(scratch),
        compiler_params=pltpu.CompilerParams(vmem_limit_bytes=kernel_room()),
        cost_estimate=pl.CostEstimate(flops=flops, bytes_accessed=nbytes, transcendentals=0),
        name=name,
    )(*args)


def tables_body(length_ref, place, gain_ref, cos_ref, sin_ref):
    rows, size = cos_ref.shape
    half = size // 2
    lane = lax.broadcasted_iota(jnp.int32, (rows, size), 1)
    row = lax.broadcasted_iota(jnp.int32, (rows, size), 0)
    index = jnp.where(lane < half, lane, lane - half).astype(F32)
    frequency = 10000.0 ** (-(index * 2.0 / size))
    angles = (length_ref[0] + row).astype(F32) * frequency
    sin = jnp.sin(angles)
    cos_ref[...] = jnp.cos(angles)
    sin_ref[...] = jnp.where(lane < half, -sin, sin)


def digits(n):
    high = n.bit_length() - 1
    out = []
    while high:
        low = max(high - 2, 0)
        out.append((low, 1 << (high - low)))
        high = low
    return out


def regroup_body(count, given, *refs):
    pieces, parts = refs[:given], refs[-count:]
    size = parts[0].shape[1]
    at = 0
    for ref in pieces:
        here = slice(at, at + ref.shape[0])
        for i, part in enumerate(parts):
            part[here] = ref[:, i * size : (i + 1) * size]
        at += ref.shape[0]


def part_shapes(n, rows, columns):
    _, count = digits(n)[0]
    return (jax.ShapeDtypeStruct((1, n // count, rows, columns), BF16),) * count


def exchange(parts, n, beside=(), other_core=False):
    levels = digits(n)
    offsets = [0]
    for level, (shift, count) in enumerate(levels):
        last = level + 1 == len(levels)
        steps = [digit << shift for digit in range(count)]
        pieces = [parts[0]] + [
            lax.ppermute(part, "wide", [(j, j ^ step) for j in range(n)])
            for step, part in zip(steps[1:], parts[1:])
        ]
        layout = [[offset ^ step for offset in offsets] for step in steps]
        offsets = sum(layout, [])
        done = list(beside[level](parts[0])) if level < len(beside) else []
        if not last:
            following = levels[level + 1][1]
            _, rest, rows, columns = pieces[0].shape
            parts = call(
                functools.partial(regroup_body, following, len(pieces)),
                (jax.ShapeDtypeStruct((len(offsets), rest // following, rows, columns), BF16),) * following,
                pieces + done,
                [IN_VMEM] * len(pieces) + [ANYWHERE] * len(done),
                name="regroup",
            )
    if not other_core:
        return pieces, layout
    other = [
        lax.ppermute(
            part, ("wide", "short"), [(2 * j + s, 2 * (j ^ step) + 1 - s) for j in range(n) for s in range(2)]
        )
        for step, part in zip(steps, parts)
    ]
    return pieces, layout, other


def place_blocks(target, at, layout, refs):
    for offsets, ref in zip(layout, refs):
        for i, offset in enumerate(offsets):
            target[at ^ offset] = ref[i, 0].astype(F32)


def join_body(*refs):
    out_ref = refs[-1]
    at = 0
    for ref in refs[:-2]:
        out_ref[at : at + ref.shape[0]] = ref[...]
        at += ref.shape[0]


def digits(n):
    high = n.bit_length() - 1
    out = []
    while high:
        low = max(high - 2, 0)
        out.append((low, 1 << (high - low)))
        high = low
    return out


def regroup_body(count, given, *refs):
    pieces, parts = refs[:given], refs[-count:]
    size = parts[0].shape[1]
    at = 0
    for ref in pieces:
        here = slice(at, at + ref.shape[0])
        for i, part in enumerate(parts):
            part[here] = ref[:, i * size : (i + 1) * size]
        at += ref.shape[0]


def part_shapes(n, rows, columns):
    _, count = digits(n)[0]
    return (jax.ShapeDtypeStruct((1, n // count, rows, columns), BF16),) * count


def exchange(parts, n, beside=(), other_core=False):
    levels = digits(n)
    offsets = [0]
    for level, (shift, count) in enumerate(levels):
        last = level + 1 == len(levels)
        steps = [digit << shift for digit in range(count)]
        pieces = [parts[0]] + [
            lax.ppermute(part, "wide", [(j, j ^ step) for j in range(n)])
            for step, part in zip(steps[1:], parts[1:])
        ]
        layout = [[offset ^ step for offset in offsets] for step in steps]
        offsets = sum(layout, [])
        done = list(beside[level](parts[0])) if level < len(beside) else []
        if not last:
            following = levels[level + 1][1]
            _, rest, rows, columns = pieces[0].shape
            parts = call(
                functools.partial(regroup_body, following, len(pieces)),
                (jax.ShapeDtypeStruct((len(offsets), rest // following, rows, columns), BF16),) * following,
                pieces + done,
                [IN_VMEM] * len(pieces) + [ANYWHERE] * len(done),
                name="regroup",
            )
    if not other_core:
        return pieces, layout
    other = [
        lax.ppermute(
            part, ("wide", "short"), [(2 * j + s, 2 * (j ^ step) + 1 - s) for j in range(n) for s in range(2)]
        )
        for step, part in zip(steps, parts)
    ]
    return pieces, layout, other


def place_blocks(target, at, layout, refs):
    for offsets, ref in zip(layout, refs):
        for i, offset in enumerate(offsets):
            target[at ^ offset] = ref[i, 0].astype(F32)


def project_body(
    shared, given, place, after, *refs
):
    x_refs, (gain_ref, wm_ref, ws_ref, wt_ref, xg_ref, send_ref, aux_ref) = refs[:given], refs[given:]
    mine = place[1]
    width = xg_ref.shape[1]
    x = jnp.concatenate(
        [ref[...].astype(F32).reshape(ref.shape[0] * ref.shape[1], width) for ref in x_refs], axis=0
    )
    squares = jnp.sum(x * x, axis=1, keepdims=True)
    xg = (x * gain_ref[...]).astype(BF16)
    xg_ref[...] = xg
    columns = wm_ref.shape[1]
    shared_at = round_up(columns, LANES)
    send_ref[:, :columns] = dot_nt(xg, wm_ref[1 - mine])
    heads = wt_ref.shape[1]
    both = dot_nt(xg, ws_ref[...])
    squares = jnp.broadcast_to(squares, (x.shape[0], LANES))
    for ref, at, group in ((send_ref, shared_at, 1 - mine), (aux_ref, 0, mine)):
        step_at = at + round_up(shared, LANES)
        ref[:, at : at + shared] = both
        ref[:, step_at : step_at + heads] = dot_nt(xg, wt_ref[group])
        ref[:, step_at + LANES :] = squares


def own_group_body(place, xg_ref, wm_ref, keep_ref):
    columns = wm_ref.shape[1]
    keep_ref[:, :columns] = dot_nt(xg_ref[...], wm_ref[place[1]])


def combine_body(width, order, keep_ref, aux_ref, recv_ref, *refs):
    parts, (inv_ref, step_ref) = refs[:-2], refs[-2:]
    rows = step_ref.shape[0]
    first = keep_ref.shape[1]
    aux = aux_ref[...] + recv_ref[:, first:]
    inv = lax.rsqrt(aux[:, -LANES:] / width + epsilon)
    inv_ref[...] = inv
    at = order.index(0) * rows
    step = aux[:, -2 * LANES : -LANES] * inv
    step_ref[...] = step[at : at + rows]
    feat = (keep_ref[...] + recv_ref[:, :first]) * inv[:, :1]
    more = aux[:, : -2 * LANES] * inv[:, :1]
    size = parts[0].shape[1]
    for i, part in enumerate(parts):
        for j in range(size):
            at = order.index(i * size + j) * rows
            part[0, j, :, :first] = feat[at : at + rows].astype(BF16)
            part[0, j, :, first:] = more[at : at + rows].astype(BF16)


def spread_blocks(wide_at, source, parts):
    size = parts[0].shape[1]
    for i, part in enumerate(parts):
        for j in range(size):
            part[0, j] = source[wide_at ^ (i * size + j)].astype(BF16)


def mixer_body(dims, layout, out_count, length_ref, place, *refs):
    feat_refs, refs = refs[: len(layout)], refs[len(layout) :]
    step_ref, cos_ref, sin_ref, bias_ref, decay_ref, skip_ref, gain_ref = refs[:7]
    key_ref, value_ref, state_ref = refs[7:10]
    parts = refs[11 : 11 + out_count]
    feat, fs, bc, own, cut = refs[11 + out_count :]
    place_blocks(feat, place[0], layout, feat_refs)
    columns, shared, shared_at, q_heads, kv_heads, heads, head_width = dims
    t_count = DRAFT_TOKENS
    hs = HEAD_SIZE
    repeat = q_heads // kv_heads
    for i in range(feat.shape[0]):
        fs[:, i * columns : (i + 1) * columns] = feat[i, :, :columns]
        bc[:, i * shared : (i + 1) * shared] = feat[i, :, shared_at : shared_at + shared]
    length = length_ref[0]

    turned = q_heads + kv_heads
    stacked = jnp.concatenate([fs[:, h * hs : (h + 1) * hs] for h in range(turned)], axis=0)
    cos = jnp.concatenate([cos_ref[...]] * turned, axis=0)
    sin = jnp.concatenate([sin_ref[...]] * turned, axis=0)
    swapped = jnp.concatenate([stacked[:, hs // 2 :], stacked[:, : hs // 2]], axis=1)
    rotated = stacked * cos + swapped * sin
    slots = key_ref.shape[0]
    scale = hs ** (-0.5)
    group_rows = repeat * t_count
    live = lax.broadcasted_iota(jnp.int32, (group_rows, slots), 1) < length
    row_t = lax.broadcasted_iota(jnp.int32, (group_rows, LANES), 0) % t_count
    causal = lax.broadcasted_iota(jnp.int32, (group_rows, LANES), 1) <= row_t
    filler = jnp.zeros((LANES - t_count, hs), F32)
    for k in range(kv_heads):
        queries = rotated[k * group_rows : (k + 1) * group_rows].astype(BF16)
        at = q_heads * t_count + k * t_count
        new_keys = jnp.concatenate([rotated[at : at + t_count], filler], axis=0).astype(BF16)
        v_at = (turned + k) * hs
        new_values = jnp.concatenate([fs[:, v_at : v_at + hs], filler], axis=0).astype(BF16)
        head = slice(k * hs, (k + 1) * hs)
        cache = jnp.where(live, dot_nt(queries, key_ref[:, head]) * scale, -1e30)
        fresh = jnp.where(causal, dot_nt(queries, new_keys) * scale, -1e30)
        highest = jnp.maximum(
            jnp.max(cache, axis=1, keepdims=True), jnp.max(fresh, axis=1, keepdims=True)
        )
        cache = jnp.exp(cache - highest)
        fresh = jnp.exp(fresh - highest)
        total = jnp.sum(cache, axis=1, keepdims=True) + jnp.sum(fresh, axis=1, keepdims=True)
        attended = dot_nn((cache / total).astype(BF16), value_ref[:, head]) + dot_nn(
            (fresh / total).astype(BF16), new_values
        )
        for r in range(repeat):
            h = k * repeat + r
            own[:, h * hs : (h + 1) * hs] = attended[r * t_count : (r + 1) * t_count]

    x_at = (turned + kv_heads) * hs
    m_size = heads * head_width
    states = bc.shape[1] // 2
    write = silu(bc[:, :states])
    read = silu(bc[:, states:])
    read_high = read.astype(BF16)
    read_low = (read - read_high.astype(F32)).astype(BF16)
    carried = dot_nt(read_high, state_ref[...]) + dot_nt(read_low, state_ref[...])
    count = heads * t_count

    def tall(v, at):
        return jnp.concatenate(
            [v[:, at + h * head_width : at + (h + 1) * head_width] for h in range(heads)], axis=0
        )

    row_head = lax.broadcasted_iota(jnp.int32, (count, heads), 0) // t_count
    mine = row_head == lax.broadcasted_iota(jnp.int32, (count, heads), 1)

    def column(v):
        if v.shape[0] > 1:
            v = jnp.concatenate([v] * heads, axis=0)
        return jnp.sum(jnp.where(mine, v, 0.0), axis=1, keepdims=True)

    wide = (count, head_width)
    token = lax.broadcasted_iota(jnp.int32, wide, 0) % t_count

    def earlier(v, d):
        moved = jnp.concatenate([v[count - d :], v[: count - d]], axis=0)
        return jnp.where(token >= d, moved, 0.0)

    raw = step_ref[:, :heads] + bias_ref[...]
    step = jnp.maximum(raw, 0.0) + jnp.log1p(jnp.exp(-jnp.abs(raw)))
    rate = jnp.broadcast_to(column(-step * decay_ref[...]), wide)
    sums = rate
    for d in range(1, t_count):
        sums = sums + earlier(rate, d)
    x = silu(tall(fs, x_at))
    gate = silu(tall(fs, x_at + m_size))
    pushed = column(step) * x
    readout = jnp.exp(sums) * tall(carried, 0) + column(skip_ref[...]) * x
    since = jnp.zeros(wide, F32)
    for d in range(t_count):
        before = write if d == 0 else jnp.concatenate([write[t_count - d :], write[: t_count - d]], axis=0)
        overlap = jnp.sum(before * read, axis=1, keepdims=True)
        overlap = jnp.concatenate([overlap] * heads, axis=0)
        if d == 0:
            readout = readout + overlap * pushed
        else:
            since = since + (rate if d == 1 else earlier(rate, d - 1))
            readout = readout + overlap * jnp.exp(since) * earlier(pushed, d)
    gated = readout * gate
    gated = gated * lax.rsqrt(jnp.mean(gated * gated, axis=1, keepdims=True) + epsilon)
    m_at = q_heads * hs
    for h in range(heads):
        at = h * head_width
        own[:, m_at + at : m_at + at + head_width] = (
            gated[h * t_count : (h + 1) * t_count] * gain_ref[:, at : at + head_width]
        )
    targets, _, piece = cut.shape
    for i in range(targets):
        cut[i] = own[:, i * piece : (i + 1) * piece]
    spread_blocks(place[0], cut, parts)


def gate_body(xg_ref, inv_ref, gate_ref, own_ref):
    def done(here, sums):
        own_ref[:, here] = sums * inv_ref[:, :1]

    blocked_dot(xg_ref, gate_ref, done)


def up_body(xg_ref, inv_ref, up_ref, gate_own_ref, after_ref, own_ref, send_ref):
    def done(here, sums):
        part = sums * inv_ref[:, :1]
        own_ref[:, here] = part
        send_ref[0, :, here] = gate_own_ref[:, here].astype(BF16)
        send_ref[1, :, here] = part.astype(BF16)

    blocked_dot(xg_ref, up_ref, done)


def down_body(gate_ref, up_ref, recv_ref, down_ref, after_ref, out_ref, hidden_ref):
    gate = gate_ref[...] + recv_ref[0].astype(F32)
    up = up_ref[...] + recv_ref[1].astype(F32)
    hidden_ref[...] = (silu(gate) * up).astype(BF16)

    def done(here, sums):
        out_ref[:, here] = sums

    blocked_dot(hidden_ref, down_ref, done)


def output_body(layout, order, place, *refs):
    count = len(layout)
    mine, other = refs[:count], refs[count : 2 * count]
    w_ref, ff_ref, out_ref = refs[2 * count :]
    wide_at, me = place[0], place[1]
    rows = out_ref.shape[1]
    senders = [offset for offsets in layout for offset in offsets]
    total = ff_ref[...]
    for part, group in ((mine, me), (other, 1 - me)):
        blocks = [ref[i, 0].astype(F32) for ref in part for i in range(ref.shape[0])]
        x = jnp.concatenate([blocks[senders.index(offset)] for offset in order], axis=0)
        total = total + dot_nn(x.astype(BF16), w_ref[group])
    for i, offset in enumerate(order):
        out_ref[wide_at ^ offset] = total[i * rows : (i + 1) * rows].astype(BF16)


def on_device(
    tokens,
    norm_gain,
    mixer_in,
    shared_in,
    step_in,
    step_bias,
    decay_rate,
    skip_gain,
    cached_keys,
    cached_values,
    lengths,
    state_cache,
    mixer_gain,
    mixer_out,
    gate_weight,
    up_weight,
    down_weight,
):
    n_short = lax.axis_size("short")
    n_wide = lax.axis_size("wide")
    own_rows, width = tokens.shape
    rows = own_rows * n_wide
    columns = mixer_in.shape[2]
    shared = shared_in.shape[1]
    heads = step_bias.shape[0]
    head_width = state_cache.shape[2]
    states = state_cache.shape[3]
    q_heads = QUERY_HEADS // n_short
    kv_heads = KEY_VALUE_HEADS // n_short
    slots = cached_keys.shape[1]
    ff = gate_weight.shape[1]
    piece = mixer_out.shape[1]
    place = jnp.stack([lax.axis_index("wide"), lax.axis_index("short")]).astype(jnp.int32)
    other_core = [(0, 1), (1, 0)]
    gain = norm_gain.reshape(1, width)

    cos, sin = call(
        tables_body,
        (jax.ShapeDtypeStruct((own_rows, HEAD_SIZE), F32), jax.ShapeDtypeStruct((own_rows, HEAD_SIZE), F32)),
        (lengths, place, gain),
        [IN_SMEM, IN_SMEM, ANYWHERE],
        flops=10**11,
        nbytes=10**8,
        name="tables",
    )

    held = tokens[None]
    offsets = [0]
    for shift, count in digits(n_wide):
        steps = [digit << shift for digit in range(1, count)]
        pieces = [held] + [
            lax.ppermute(held, "wide", [(j, j ^ step) for j in range(n_wide)]) for step in steps
        ]
        offsets = [[rel ^ step for rel in offsets] for step in [0] + steps]
        layout, offsets = offsets, sum(offsets, [])
        if shift:
            held = call(
                join_body,
                jax.ShapeDtypeStruct((len(offsets), own_rows, width), BF16),
                pieces + [cos],
                [IN_VMEM] * len(pieces) + [ANYWHERE],
                name="join",
            )
    used = round_up(columns, LANES) + round_up(shared, LANES)
    sent = used + 2 * LANES
    wm = jnp.transpose(mixer_in, (1, 2, 0))
    ws = jnp.transpose(shared_in)
    wt = jnp.transpose(step_in).reshape(n_short, heads, width)
    weights = (wm.size + ws.size + wt.size) * 2
    order = sum(layout, [])
    xg, send, aux = call(
        functools.partial(project_body, shared, len(pieces)),
        (
            jax.ShapeDtypeStruct((rows, width), BF16),
            jax.ShapeDtypeStruct((rows, sent), F32),
            jax.ShapeDtypeStruct((rows, sent - round_up(columns, LANES)), F32),
        ),
        (place, cos, *pieces, gain, wm, ws, wt),
        [IN_SMEM, ANYWHERE] + [IN_VMEM] * (len(pieces) + 4),
        flops=rows * weights,
        nbytes=20 * weights,
        name="project",
    )
    received = lax.ppermute(send, "short", other_core)
    keep = call(
        own_group_body,
        jax.ShapeDtypeStruct((rows, round_up(columns, LANES)), F32),
        (place, xg, wm),
        [IN_SMEM, IN_VMEM, IN_VMEM],
        flops=rows * weights,
        nbytes=weights // 2,
        name="own_group",
    )
    *parts, inv, step_raw = call(
        functools.partial(combine_body, width * n_short, order),
        part_shapes(n_wide, own_rows, used)
        + (
            jax.ShapeDtypeStruct((rows, LANES), F32),
            jax.ShapeDtypeStruct((own_rows, LANES), F32),
        ),
        (keep, aux, received),
        [IN_VMEM] * 3,
        flops=4 * rows * sent,
        nbytes=8 * rows * sent,
        name="combine",
    )
    made = []

    def gate(after):
        made.append(
            call(
                gate_body,
                jax.ShapeDtypeStruct((rows, ff), F32),
                (xg, inv, gate_weight),
                [IN_VMEM] * 3,
                flops=2 * rows * width * ff,
                nbytes=2 * width * ff,
                name="gate",
            )
        )
        return made

    def up(after):
        made.extend(
            call(
                up_body,
                (jax.ShapeDtypeStruct((rows, ff), F32), jax.ShapeDtypeStruct((2, rows, ff), BF16)),
                (xg, inv, up_weight, made[0], after),
                [IN_VMEM] * 4 + [ANYWHERE],
                flops=2 * rows * width * ff,
                nbytes=2 * width * ff,
                name="up",
            )
        )
        return made[1:]

    features, layout = exchange(parts, n_wide, (gate, up))
    gate_own, up_own, ff_send = made
    features, ff_send = lax.optimization_barrier((features, ff_send))
    ff_received = lax.ppermute(ff_send, "short", other_core)
    out_shapes = part_shapes(n_wide, own_rows, piece)
    parts = call(
        functools.partial(
            mixer_body,
            (columns, shared, round_up(columns, LANES), q_heads, kv_heads, heads, head_width),
            layout,
            len(out_shapes),
        ),
        out_shapes,
        (
            lengths,
            place,
            *features,
            step_raw,
            cos,
            sin,
            step_bias.reshape(1, heads),
            decay_rate.reshape(1, heads),
            skip_gain.reshape(1, heads),
            mixer_gain.reshape(1, heads * head_width),
            cached_keys[0],
            cached_values[0],
            state_cache.reshape(heads * head_width, states),
            up_own,
        ),
        [IN_SMEM] * 2 + [IN_VMEM] * (len(features) + 10) + [ANYWHERE],
        [
            pltpu.VMEM((n_wide, own_rows, used), F32),
            pltpu.VMEM((own_rows, n_wide * columns), F32),
            pltpu.VMEM((own_rows, n_wide * shared), F32),
            pltpu.VMEM((own_rows, n_wide * piece), F32),
            pltpu.VMEM((n_wide, own_rows, piece), F32),
        ],
        flops=4 * own_rows * state_cache.size,
        nbytes=6 * state_cache.size,
        name="mixers",
    )
    ff_out = []

    def down(after):
        ff_out.append(
            call(
                down_body,
                jax.ShapeDtypeStruct((rows, width), F32),
                (gate_own, up_own, ff_received, down_weight, after),
                [IN_VMEM] * 4 + [ANYWHERE],
                [pltpu.VMEM((rows, ff), BF16)],
                flops=2 * rows * width * ff,
                nbytes=2 * width * ff,
                name="down",
            )
        )
        return ff_out

    mine, layout, other = exchange(parts, n_wide, (down,), other_core=True)
    summed = call(
        functools.partial(output_body, layout, order),
        jax.ShapeDtypeStruct((n_wide, own_rows, width), BF16),
        (place, *mine, *other, mixer_out, ff_out[0]),
        [IN_SMEM] + [IN_VMEM] * (2 * len(mine) + 2),
        flops=4 * rows * width * piece,
        nbytes=4 * width * piece,
        name="output",
    )
    pieces = lax.all_to_all(summed, "wide", split_axis=0, concat_axis=0, tiled=True)
    total = tokens.astype(F32) + jnp.sum(pieces.astype(F32), axis=0)
    return total.astype(BF16)


def solution(mesh):
    in_specs = (
        P(("groups", "wide"), "short"),
        P("short"),
        P("short", None, "wide"),
        P("short", "wide"),
        P("short", None),
        P("short"),
        P("short"),
        P("short"),
        P(("groups", "wide"), None, "short"),
        P(("groups", "wide"), None, "short"),
        P(("groups", "wide")),
        P(("groups", "wide"), "short", None, None),
        P("short"),
        P(None, "wide", "short"),
        P("short", "wide"),
        P("short", "wide"),
        P("wide", "short"),
    )
    out_specs = P(("groups", "wide"), "short")
    return jax.shard_map(
        on_device, mesh=mesh, in_specs=in_specs, out_specs=out_specs, check_vma=False
    )
```

time: 87.5 us -> 58.7 us (0.67)
  local copies, waits for them, and re-layouts: 20.5 us -> 0.86 us
  blocking collectives: 19.9 us -> 10.4 us
  starting transfers between devices: 14.5 us -> 19.7 us
  other arithmetic: 3.37 us -> 0.78 us
  waiting for transfers between devices: 13.3 us -> 11.4 us
    unnamed x32 -> x50, local copies, waits for them, and re-layouts: 19.8 us -> 0.15 us
    ppermute x4 -> x14, starting transfers between devices: 7.98 us -> 19.7 us  [the longest x8 10.9 us: exchange(): lax.ppermute(part, 'wide', [(j, j ^ step) for j in range(n)])]
    all_to_all x1 -> x0, blocking collectives: 9.06 us -> none  [on_device(): lax.all_to_all(mixed_rows, 'wide', split_axis=0, concat_axis=0, tiled=True)]
    all_to_all x1 -> x0, waiting for transfers between devices: 6.77 us -> none  [on_device(): lax.all_to_all(features, 'wide', split_axis=0, concat_axis=0, tiled=True)]
    all_to_all x1 -> x0, starting transfers between devices: 6.26 us -> none  [on_device(): lax.all_to_all(features, 'wide', split_axis=0, concat_axis=0, tiled=True)]
    ppermute x4 -> x14, waiting for transfers between devices: 5.83 us -> 11.4 us  [the longest x4 5.17 us: on_device(): lax.ppermute(held, 'wide', [(j, j ^ step) for j in range(n_wide)])]
    concatenate x4 -> x0, other arithmetic: 2.47 us -> none  [the longest x3 2.39 us: on_device(): gathered = jnp.concatenate([gathered, moved], axis=0)]
    pallas_call x6 -> x12, Pallas kernels: 14.4 us -> 14.2 us  [call(): pl.pallas_call(body, out_shape=out_shape, in_specs=specs, out_specs=outs,...]
  transfers between devices with their start and end apart: 7 -> 16, of which waited for: 5 -> 7; matrix products, arithmetic and copies ran while one was open for 1% -> 1% of each run, Pallas kernels for 5% -> 18%
where the time goes in v2:
time: 58.7 us; the launch traced here: 58.4 us
  starting transfers between devices  19.7 us (34%)
  Pallas kernels  14.2 us (24%)
  waiting for transfers between devices  11.4 us (19%)
  blocking collectives  10.4 us (18%)
  between operations  1.06 us (2%)
  local copies, waits for them, and re-layouts  0.86 us (1%)
  other arithmetic  0.78 us (1%)
    pallas_call x12, Pallas kernels, call(): pl.pallas_call(body, out_shape=out_shape, in_specs=specs, out_specs=outs,...  14.2 us
    ppermute x8, starting transfers between devices, exchange(): lax.ppermute(part, 'wide', [(j, j ^ step) for j in range(n)])  10.9 us
    all_to_all x1, blocking collectives, on_device(): lax.all_to_all(summed, 'wide', split_axis=0, concat_axis=0, tiled=True)  10.4 us
    ppermute x4, starting transfers between devices, on_device(): lax.ppermute(held, 'wide', [(j, j ^ step) for j in range(n_wide)])  7.17 us
    ppermute x4, waiting for transfers between devices, on_device(): lax.ppermute(held, 'wide', [(j, j ^ step) for j in range(n_wide)])  5.17 us
    ppermute x8, waiting for transfers between devices, exchange(): lax.ppermute(part, 'wide', [(j, j ^ step) for j in range(n)])  5.14 us
    ppermute x2, starting transfers between devices, exchange(): lax.ppermute(part, ('wide', 'short'), [(2 * j + s, 2 * (j ^ step) + 1 - s...  1.6 us
  transfers between devices with their start and end apart: 16, of which 7 were waited for; matrix products, arithmetic and copies ran while one was open for 1% of the time, Pallas kernels for 18%

profile of v2, /device:TPU:0, one launch (start us, length us, event | category | flops | bytes accessed | tf_op | source)
XLA Modules:
  0.0 58.4 jit_solution(2727993739603620904)
XLA Ops:
  0.0 5.0 %collective-permute-start.2 = (bf16[1,4,2560]{2,1,0:T(4,128)(2,1)}, bf16[1,4,2560]{2,1,0:T(4,128)(2,1)S(1)}, u32[]{:S(2)}, u32[]{:S(2)}) collective-permute-start(bf16[1,4,2560]{2,1,0:T(4,128)(2,1)} %bitcast.30), channel_id=1, source_target_pairs={{0,12},{2,14},{4,8},{6,10},{8,4},{10,6},{12,0},{14,2},{1,13},{3,15... | collective-permute-start | bytes 61448 | tf_op jit(solution)/shard_map/ppermute | solution.py:495
  6.3 0.7 %reshape.21.gain_ref.refs_2_ = f32[1,2560]{1,0:T(1,128)S(1)} reshape(f32[2560]{0:T(1024)} %param.18) | data formatting | bytes 20480 | tf_op jit(solution)/shard_map/reshape | solution.py:478
  7.7 2.2 %collective-permute-done.1.refs_2_ = bf16[1,4,2560]{2,1,0:T(4,128)(2,1)S(1)} collective-permute-done((bf16[1,4,2560]{2,1,0:T(4,128)(2,1)}, bf16[1,4,2560]{2,1,0:T(4,128)(2,1)S(1)}, u32[]{:S(2)}, u32[]{:S(2)}) %collective-permute-start.1) | collective-permute-done | bytes 20512 | tf_op jit(solution)/shard_map/ppermute | solution.py:495
  10.0 1.6 %collective-permute-start.3 = (bf16[4,4,2560]{2,1,0:T(4,128)(2,1)S(1)}, bf16[4,4,2560]{2,1,0:T(4,128)(2,1)S(1)}, u32[]{:S(2)}, u32[]{:S(2)}) collective-permute-start(bf16[4,4,2560]{2,1,0:T(4,128)(2,1)S(1)} %join.1.refs_0_), channel_id=1, source_target_pairs={{0,2},{2,0},{4,6},{6,4},{8,10},{10,8},{12,14},{14,12},{1,3},{3,1},... | collective-permute-start | bytes 245768 | tf_op jit(solution)/shard_map/ppermute | solution.py:495
  11.5 2.9 %collective-permute-done.3.refs_1_ = bf16[4,4,2560]{2,1,0:T(4,128)(2,1)S(1)} collective-permute-done((bf16[4,4,2560]{2,1,0:T(4,128)(2,1)S(1)}, bf16[4,4,2560]{2,1,0:T(4,128)(2,1)S(1)}, u32[]{:S(2)}, u32[]{:S(2)}) %collective-permute-start.3) | collective-permute-done | bytes 81952 | tf_op jit(solution)/shard_map/ppermute | solution.py:495
  14.5 1.9 %project.1 = (bf16[32,2560]{1,0:T(8,128)(2,1)S(1)}, f32[32,1152]{1,0:T(8,128)S(1)}, f32[32,384]{1,0:T(8,128)S(1)}) custom-call(s32[2]{0:T(128)S(1)} %pad_add_fusion.place, f32[4,128]{1,0:T(4,128)S(1)} %get-tuple-element.29.refs_4_.after.refs_3_, bf16[4,4,2560]{2,1,0:T(4,128)(2,1)S(1)} %join.1.refs_0_, ...), custom_call_target="tpu_custom_call" | custom-call | flops 256901120 | bytes 160563200 | tf_op jit(solution)/shard_map/project/pallas_call | solution.py:62
  16.5 1.7 %own_group.1.keep_ref = f32[32,768]{1,0:T(8,128)S(1)} custom-call(s32[2]{0:T(128)S(1)} %pad_add_fusion.place, bf16[32,2560]{1,0:T(8,128)(2,1)S(1)} %get-tuple-element.30.xg_ref, bf16[2,736,2560]{2,1,0:T(8,128)(2,1)S(1)} %bitcast.16), custom_call_target="tpu_custom_call" | custom-call | flops 256901120 | bytes 4014080 | tf_op jit(solution)/shard_map/own_group/pallas_call | solution.py:62
  18.4 2.3 %collective-permute-start.6 = (bf16[1,2,4,896]{3,2,1,0:T(4,128)(2,1)S(1)}, bf16[1,2,4,896]{3,2,1,0:T(4,128)(2,1)S(1)}, u32[]{:S(2)}, u32[]{:S(2)}) collective-permute-start(bf16[1,2,4,896]{3,2,1,0:T(4,128)(2,1)S(1)} %get-tuple-element.35), channel_id=1, source_target_pairs={{0,8},{2,10},{4,12},{6,14},{8,0},{10,2},{12,4},{14,6},{1,9},{3,11}... | collective-permute-start | bytes 43016 | tf_op jit(solution)/shard_map/ppermute | solution.py:194
  20.7 2.1 %collective-permute-start.7 = (bf16[1,2,4,896]{3,2,1,0:T(4,128)(2,1)S(1)}, bf16[1,2,4,896]{3,2,1,0:T(4,128)(2,1)S(1)}, u32[]{:S(2)}, u32[]{:S(2)}) collective-permute-start(bf16[1,2,4,896]{3,2,1,0:T(4,128)(2,1)S(1)} %get-tuple-element.36), channel_id=1, source_target_pairs={{0,12},{2,14},{4,8},{6,10},{8,4},{10,6},{12,0},{14,2},{1,13},{3,15... | collective-permute-start | bytes 43016 | tf_op jit(solution)/shard_map/ppermute | solution.py:194
  22.9 2.1 %gate.1.refs_4_.gate_own_ref.gate_ref = f32[32,2688]{1,0:T(8,128)S(1)} custom-call(bf16[32,2560]{1,0:T(8,128)(2,1)S(1)} %get-tuple-element.30.xg_ref, f32[32,128]{1,0:T(8,128)S(1)} %get-tuple-element.37.inv_ref, bf16[2560,2688]{1,0:T(8,128)(2,1)S(1)} %bitcast.18), custom_call_target="tpu_custom_call" | custom-call | flops 440401920 | bytes 13762560 | tf_op jit(solution)/shard_map/gate/pallas_call | solution.py:62
  25.0 1.2 %collective-permute-done.7.refs_3_ = bf16[1,2,4,896]{3,2,1,0:T(4,128)(2,1)S(1)} collective-permute-done((bf16[1,2,4,896]{3,2,1,0:T(4,128)(2,1)S(1)}, bf16[1,2,4,896]{3,2,1,0:T(4,128)(2,1)S(1)}, u32[]{:S(2)}, u32[]{:S(2)}) %collective-permute-start.7) | collective-permute-done | bytes 14368 | tf_op jit(solution)/shard_map/ppermute | solution.py:194
  26.2 1.5 %collective-permute-start.8 = (bf16[4,1,4,896]{3,2,1,0:T(4,128)(2,1)S(1)}, bf16[4,1,4,896]{3,2,1,0:T(4,128)(2,1)S(1)}, u32[]{:S(2)}, u32[]{:S(2)}) collective-permute-start(bf16[4,1,4,896]{3,2,1,0:T(4,128)(2,1)S(1)} %get-tuple-element.39), channel_id=1, source_target_pairs={{0,2},{2,0},{4,6},{6,4},{8,10},{10,8},{12,14},{14,12},{1,3},{3,1},... | collective-permute-start | bytes 86024 | tf_op jit(solution)/shard_map/ppermute | solution.py:194
  27.7 2.1 %up.1 = (f32[32,2688]{1,0:T(8,128)S(1)}, bf16[2,32,2688]{2,1,0:T(8,128)(2,1)S(1)}) custom-call(bf16[32,2560]{1,0:T(8,128)(2,1)S(1)} %get-tuple-element.30.xg_ref, f32[32,128]{1,0:T(8,128)S(1)} %get-tuple-element.37.inv_ref, bf16[2560,2688]{1,0:T(8,128)(2,1)S(1)} %bitcast.20, f32[32,2688]{1,0:T(8,128)S(1)} %gate.1.refs_4_.gate_own_ref.gate_ref, ...), custom_call_target="tpu_custom_call" | custom-call | flops 440401920 | bytes 13762560 | tf_op jit(solution)/shard_map/up/pallas_call | solution.py:62
  30.1 2.3 %mixers.1 = (bf16[1,2,4,416]{3,2,1,0:T(4,128)(2,1)S(1)}, bf16[1,2,4,416]{3,2,1,0:T(4,128)(2,1)S(1)}, bf16[1,2,4,416]{3,2,1,0:T(4,128)(2,1)S(1)}, bf16[1,2,4,416]{3,2,1,0:T(4,128)(2,1)S(1)}) custom-call(s32[1]{0:T(128)S(6)} %copy.18.length_ref, s32[2]{0:T(128)S(1)} %pad_add_fusion.place, bf16[4,1,4,896]{3,2,1,0:T(4,128)(2,1)S(1)} %get-tuple-element.41.after_ref.refs_0_, ...), custom_call_target="tpu_custom_call" | custom-call | flops 8388608 | bytes 3145728 | tf_op jit(solution)/shard_map/mixers/pallas_call | solution.py:62
  32.5 2.6 %collective-permute-start.10 = (bf16[1,2,4,416]{3,2,1,0:T(4,128)(2,1)S(1)}, bf16[1,2,4,416]{3,2,1,0:T(4,128)(2,1)S(1)}, u32[]{:S(2)}, u32[]{:S(2)}) collective-permute-start(bf16[1,2,4,416]{3,2,1,0:T(4,128)(2,1)S(1)} %get-tuple-element.48), channel_id=1, source_target_pairs={{0,8},{2,10},{4,12},{6,14},{8,0},{10,2},{12,4},{14,6},{1,9},{3,11}... | collective-permute-start | bytes 19976 | tf_op jit(solution)/shard_map/ppermute | solution.py:194
  35.1 1.7 %collective-permute-start.11 = (bf16[1,2,4,416]{3,2,1,0:T(4,128)(2,1)S(1)}, bf16[1,2,4,416]{3,2,1,0:T(4,128)(2,1)S(1)}, u32[]{:S(2)}, u32[]{:S(2)}) collective-permute-start(bf16[1,2,4,416]{3,2,1,0:T(4,128)(2,1)S(1)} %get-tuple-element.49), channel_id=1, source_target_pairs={{0,12},{2,14},{4,8},{6,10},{8,4},{10,6},{12,0},{14,2},{1,13},{3,15... | collective-permute-start | bytes 19976 | tf_op jit(solution)/shard_map/ppermute | solution.py:194
  36.9 2.0 %down.1.refs_4_.refs_5_ = f32[32,2560]{1,0:T(8,128)S(1)} custom-call(f32[32,2688]{1,0:T(8,128)S(1)} %gate.1.refs_4_.gate_own_ref.gate_ref, f32[32,2688]{1,0:T(8,128)S(1)} %get-tuple-element.45.refs_12_.up_ref, bf16[2,32,2688]{2,1,0:T(8,128)(2,1)S(1)} %collective-permute-done.12.recv_ref, bf16[2688,2560]{1,0:T(8,128)(2,1)S(1)} %bitcast.22, ...), custom_call_target="tpu_custom_call" | custom-call | flops 440401920 | bytes 13762560 | tf_op jit(solution)/shard_map/down/pallas_call | solution.py:62
  38.9 1.6 %collective-permute-done.11.refs_3_ = bf16[1,2,4,416]{3,2,1,0:T(4,128)(2,1)S(1)} collective-permute-done((bf16[1,2,4,416]{3,2,1,0:T(4,128)(2,1)S(1)}, bf16[1,2,4,416]{3,2,1,0:T(4,128)(2,1)S(1)}, u32[]{:S(2)}, u32[]{:S(2)}) %collective-permute-start.11) | collective-permute-done | bytes 6688 | tf_op jit(solution)/shard_map/ppermute | solution.py:194
  40.6 1.6 %collective-permute-start.15 = (bf16[4,1,4,416]{3,2,1,0:T(4,128)(2,1)S(1)}, bf16[4,1,4,416]{3,2,1,0:T(4,128)(2,1)S(1)}, u32[]{:S(2)}, u32[]{:S(2)}) collective-permute-start(bf16[4,1,4,416]{3,2,1,0:T(4,128)(2,1)S(1)} %get-tuple-element.52), channel_id=1, source_target_pairs={{0,3},{1,2},{2,1},{3,0},{4,7},{5,6},{6,5},{7,4},{8,11},{9,10},{10,... | collective-permute-start | bytes 39944 | tf_op jit(solution)/shard_map/ppermute | solution.py:213
  42.7 1.1 %collective-permute-done.15.refs_3_ = bf16[4,1,4,416]{3,2,1,0:T(4,128)(2,1)S(1)} collective-permute-done((bf16[4,1,4,416]{3,2,1,0:T(4,128)(2,1)S(1)}, bf16[4,1,4,416]{3,2,1,0:T(4,128)(2,1)S(1)}, u32[]{:S(2)}, u32[]{:S(2)}) %collective-permute-start.15) | collective-permute-done | bytes 13344 | tf_op jit(solution)/shard_map/ppermute | solution.py:213
  43.8 2.1 %collective-permute-done.13.refs_1_ = bf16[4,1,4,416]{3,2,1,0:T(4,128)(2,1)S(1)} collective-permute-done((bf16[4,1,4,416]{3,2,1,0:T(4,128)(2,1)S(1)}, bf16[4,1,4,416]{3,2,1,0:T(4,128)(2,1)S(1)}, u32[]{:S(2)}, u32[]{:S(2)}) %collective-permute-start.13) | collective-permute-done | bytes 13344 | tf_op jit(solution)/shard_map/ppermute | solution.py:194
  45.9 1.4 %output.1 = bf16[8,4,2560]{2,1,0:T(4,128)(2,1)S(1)} custom-call(s32[2]{0:T(128)S(1)} %pad_add_fusion.place, bf16[4,1,4,416]{3,2,1,0:T(4,128)(2,1)S(1)} %get-tuple-element.51.refs_0_, bf16[4,1,4,416]{3,2,1,0:T(4,128)(2,1)S(1)} %collective-permute-done.13.refs_1_, bf16[4,1,4,416]{3,2,1,0:T(4,128)(2,1)S(1)} %collective-permute-done.14.refs_2_, ...), custom_call_target="tpu_custom_call" | custom-call | flops 136314880 | bytes 4259840 | tf_op jit(solution)/shard_map/output/pallas_call | solution.py:62
  47.3 10.4 %all_to_all.5 = bf16[8,4,2560]{2,1,0:T(4,128)(2,1)S(1)} all-to-all(bf16[8,4,2560]{2,1,0:T(4,128)(2,1)S(1)} %output.1), channel_id=1, replica_groups=mesh['groups'=2,'wide'=8,'short'=2] {'wide'}, dimensions={0} | all-to-all | bytes 327680 | tf_op jit(solution)/shard_map/all_to_all | solution.py:648
  57.8 0.6 %add_convert_fusion = bf16[4,2560]{1,0:T(4,128)(2,1)} fusion(f32[4,2560]{1,0:T(4,128)S(1)} %convert_reduce_fusion, bf16[4,2560]{1,0:T(4,128)(2,1)S(1)} %copy-done.6), kind=kLoop, calls=%fused_computation.1 | loop fusion | flops 30720 | bytes 81920 | tf_op jit(solution)/shard_map/convert_element_type | solution.py:650
  (79 shorter events, 2.6 us)
Async XLA Ops:
  0.0 7.7 %collective-permute-start.2 = (bf16[1,4,2560]{2,1,0:T(4,128)(2,1)}, bf16[1,4,2560]{2,1,0:T(4,128)(2,1)S(1)}, u32[]{:S(2)}, u32[]{:S(2)}) collective-permute-start(bf16[1,4,2560]{2,1,0:T(4,128)(2,1)} %bitcast.30), channel_id=1, source_target_pairs={{0,12},{2,14},{4,8},{6,10},{8,4},{10,6},{12,0},{14,2},{1,13},{3,15... | collective-permute-start | bytes 61448 | tf_op jit(solution)/shard_map/ppermute | solution.py:495
  5.0 4.9 %collective-permute-start.1 = (bf16[1,4,2560]{2,1,0:T(4,128)(2,1)}, bf16[1,4,2560]{2,1,0:T(4,128)(2,1)S(1)}, u32[]{:S(2)}, u32[]{:S(2)}) collective-permute-start(bf16[1,4,2560]{2,1,0:T(4,128)(2,1)} %bitcast.31), channel_id=1, source_target_pairs={{0,8},{2,10},{4,12},{6,14},{8,0},{10,2},{12,4},{14,6},{1,9},{3,11}... | collective-permute-start | bytes 61448 | tf_op jit(solution)/shard_map/ppermute | solution.py:495
  5.1 4.9 %collective-permute-start = (bf16[1,4,2560]{2,1,0:T(4,128)(2,1)}, bf16[1,4,2560]{2,1,0:T(4,128)(2,1)S(1)}, u32[]{:S(2)}, u32[]{:S(2)}) collective-permute-start(bf16[1,4,2560]{2,1,0:T(4,128)(2,1)} %bitcast.32), channel_id=1, source_target_pairs={{0,4},{2,6},{4,0},{6,2},{8,12},{10,14},{12,8},{14,10},{1,5},{3,7},... | collective-permute-start | bytes 61448 | tf_op jit(solution)/shard_map/ppermute | solution.py:495
  7.0 15.8 %slice-start = ((s8[13762560]{0:T(1024)(128)(4,1)}), s8[4194304]{0:T(1024)(128)(4,1)S(1)}, s32[]{:S(2)}) async-start(s8[13762560]{0:T(1024)(128)(4,1)} %bitcast.17), calls=%async_computation.1 | async-start | bytes 8388608
  7.1 15.7 %slice-start.1 = ((s8[13762560]{0:T(1024)(128)(4,1)}), s8[4194304]{0:T(1024)(128)(4,1)S(1)}, s32[]{:S(2)}) async-start(s8[13762560]{0:T(1024)(128)(4,1)} %bitcast.17), calls=%async_computation.2 | async-start | bytes 8388608
  7.1 15.6 %slice-start.2 = ((s8[13762560]{0:T(1024)(128)(4,1)}), s8[4194304]{0:T(1024)(128)(4,1)S(1)}, s32[]{:S(2)}) async-start(s8[13762560]{0:T(1024)(128)(4,1)} %bitcast.17), calls=%async_computation.3 | async-start | bytes 8388608
  7.1 15.6 %slice-start.3 = ((s8[13762560]{0:T(1024)(128)(4,1)}), s8[1179648]{0:T(1024)(128)(4,1)S(1)}, s32[]{:S(2)}) async-start(s8[13762560]{0:T(1024)(128)(4,1)} %bitcast.17), calls=%async_computation.4 | async-start | bytes 2359296
  10.0 4.5 %collective-permute-start.3 = (bf16[4,4,2560]{2,1,0:T(4,128)(2,1)S(1)}, bf16[4,4,2560]{2,1,0:T(4,128)(2,1)S(1)}, u32[]{:S(2)}, u32[]{:S(2)}) collective-permute-start(bf16[4,4,2560]{2,1,0:T(4,128)(2,1)S(1)} %join.1.refs_0_), channel_id=1, source_target_pairs={{0,2},{2,0},{4,6},{6,4},{8,10},{10,8},{12,14},{14,12},{1,3},{3,1},... | collective-permute-start | bytes 245768 | tf_op jit(solution)/shard_map/ppermute | solution.py:495
  16.4 1.8 %collective-permute-start.4 = (f32[32,1152]{1,0:T(8,128)S(1)}, f32[32,1152]{1,0:T(8,128)S(1)}, u32[]{:S(2)}, u32[]{:S(2)}) collective-permute-start(f32[32,1152]{1,0:T(8,128)S(1)} %get-tuple-element.32), channel_id=1, source_target_pairs={{0,1},{1,0},{2,3},{3,2},{4,5},{5,4},{6,7},{7,6},{8,9},{9,8},{10,11... | collective-permute-start | bytes 442376 | tf_op jit(solution)/shard_map/ppermute | solution.py:527
  18.3 6.7 %collective-permute-start.5 = (bf16[1,2,4,896]{3,2,1,0:T(4,128)(2,1)S(1)}, bf16[1,2,4,896]{3,2,1,0:T(4,128)(2,1)S(1)}, u32[]{:S(2)}, u32[]{:S(2)}) collective-permute-start(bf16[1,2,4,896]{3,2,1,0:T(4,128)(2,1)S(1)} %get-tuple-element.34), channel_id=1, source_target_pairs={{0,4},{2,6},{4,0},{6,2},{8,12},{10,14},{12,8},{14,10},{1,5},{3,7},... | collective-permute-start | bytes 43016 | tf_op jit(solution)/shard_map/ppermute | solution.py:194
  18.4 6.6 %collective-permute-start.6 = (bf16[1,2,4,896]{3,2,1,0:T(4,128)(2,1)S(1)}, bf16[1,2,4,896]{3,2,1,0:T(4,128)(2,1)S(1)}, u32[]{:S(2)}, u32[]{:S(2)}) collective-permute-start(bf16[1,2,4,896]{3,2,1,0:T(4,128)(2,1)S(1)} %get-tuple-element.35), channel_id=1, source_target_pairs={{0,8},{2,10},{4,12},{6,14},{8,0},{10,2},{12,4},{14,6},{1,9},{3,11}... | collective-permute-start | bytes 43016 | tf_op jit(solution)/shard_map/ppermute | solution.py:194
  20.7 5.5 %collective-permute-start.7 = (bf16[1,2,4,896]{3,2,1,0:T(4,128)(2,1)S(1)}, bf16[1,2,4,896]{3,2,1,0:T(4,128)(2,1)S(1)}, u32[]{:S(2)}, u32[]{:S(2)}) collective-permute-start(bf16[1,2,4,896]{3,2,1,0:T(4,128)(2,1)S(1)} %get-tuple-element.36), channel_id=1, source_target_pairs={{0,12},{2,14},{4,8},{6,10},{8,4},{10,6},{12,0},{14,2},{1,13},{3,15... | collective-permute-start | bytes 43016 | tf_op jit(solution)/shard_map/ppermute | solution.py:194
  22.9 14.0 %slice-start.8 = ((s8[13762560]{0:T(1024)(128)(4,1)}), s8[4194304]{0:T(1024)(128)(4,1)S(1)}, s32[]{:S(2)}) async-start(s8[13762560]{0:T(1024)(128)(4,1)} %bitcast.21), calls=%async_computation.9 | async-start | bytes 8388608
  22.9 14.0 %slice-start.9 = ((s8[13762560]{0:T(1024)(128)(4,1)}), s8[4194304]{0:T(1024)(128)(4,1)S(1)}, s32[]{:S(2)}) async-start(s8[13762560]{0:T(1024)(128)(4,1)} %bitcast.21), calls=%async_computation.10 | async-start | bytes 8388608
  26.2 3.9 %collective-permute-start.8 = (bf16[4,1,4,896]{3,2,1,0:T(4,128)(2,1)S(1)}, bf16[4,1,4,896]{3,2,1,0:T(4,128)(2,1)S(1)}, u32[]{:S(2)}, u32[]{:S(2)}) collective-permute-start(bf16[4,1,4,896]{3,2,1,0:T(4,128)(2,1)S(1)} %get-tuple-element.39), channel_id=1, source_target_pairs={{0,2},{2,0},{4,6},{6,4},{8,10},{10,8},{12,14},{14,12},{1,3},{3,1},... | collective-permute-start | bytes 86024 | tf_op jit(solution)/shard_map/ppermute | solution.py:194
  27.7 18.2 %slice-start.12 = ((s8[4259840]{0:T(1024)(128)(4,1)}), s8[4194304]{0:T(1024)(128)(4,1)S(1)}, s32[]{:S(2)}) async-start(s8[4259840]{0:T(1024)(128)(4,1)} %bitcast.23), calls=%async_computation.13 | async-start | bytes 8388608
  30.1 6.8 %collective-permute-start.12 = (bf16[2,32,2688]{2,1,0:T(8,128)(2,1)S(1)}, bf16[2,32,2688]{2,1,0:T(8,128)(2,1)S(1)}, u32[]{:S(2)}, u32[]{:S(2)}) collective-permute-start(bf16[2,32,2688]{2,1,0:T(8,128)(2,1)S(1)} %get-tuple-element.50), channel_id=1, source_target_pairs={{0,1},{1,0},{2,3},{3,2},{4,5},{5,4},{6,7},{7,6},{8,9},{9,8},{10,11... | collective-permute-start | bytes 1032200 | tf_op jit(solution)/shard_map/ppermute | solution.py:583
  30.1 15.8 %slice-start.13 = ((s8[4259840]{0:T(1024)(128)(4,1)}), s8[65536]{0:T(1024)(128)(4,1)S(1)}, s32[]{:S(2)}) async-start(s8[4259840]{0:T(1024)(128)(4,1)} %bitcast.23), calls=%async_computation.14 | async-start | bytes 131072
  32.4 6.5 %collective-permute-start.9 = (bf16[1,2,4,416]{3,2,1,0:T(4,128)(2,1)S(1)}, bf16[1,2,4,416]{3,2,1,0:T(4,128)(2,1)S(1)}, u32[]{:S(2)}, u32[]{:S(2)}) collective-permute-start(bf16[1,2,4,416]{3,2,1,0:T(4,128)(2,1)S(1)} %get-tuple-element.47), channel_id=1, source_target_pairs={{0,4},{2,6},{4,0},{6,2},{8,12},{10,14},{12,8},{14,10},{1,5},{3,7},... | collective-permute-start | bytes 19976 | tf_op jit(solution)/shard_map/ppermute | solution.py:194
  32.5 6.4 %collective-permute-start.10 = (bf16[1,2,4,416]{3,2,1,0:T(4,128)(2,1)S(1)}, bf16[1,2,4,416]{3,2,1,0:T(4,128)(2,1)S(1)}, u32[]{:S(2)}, u32[]{:S(2)}) collective-permute-start(bf16[1,2,4,416]{3,2,1,0:T(4,128)(2,1)S(1)} %get-tuple-element.48), channel_id=1, source_target_pairs={{0,8},{2,10},{4,12},{6,14},{8,0},{10,2},{12,4},{14,6},{1,9},{3,11}... | collective-permute-start | bytes 19976 | tf_op jit(solution)/shard_map/ppermute | solution.py:194
  35.1 5.4 %collective-permute-start.11 = (bf16[1,2,4,416]{3,2,1,0:T(4,128)(2,1)S(1)}, bf16[1,2,4,416]{3,2,1,0:T(4,128)(2,1)S(1)}, u32[]{:S(2)}, u32[]{:S(2)}) collective-permute-start(bf16[1,2,4,416]{3,2,1,0:T(4,128)(2,1)S(1)} %get-tuple-element.49), channel_id=1, source_target_pairs={{0,12},{2,14},{4,8},{6,10},{8,4},{10,6},{12,0},{14,2},{1,13},{3,15... | collective-permute-start | bytes 19976 | tf_op jit(solution)/shard_map/ppermute | solution.py:194
  40.6 2.1 %collective-permute-start.14 = (bf16[4,1,4,416]{3,2,1,0:T(4,128)(2,1)S(1)}, bf16[4,1,4,416]{3,2,1,0:T(4,128)(2,1)S(1)}, u32[]{:S(2)}, u32[]{:S(2)}) collective-permute-start(bf16[4,1,4,416]{3,2,1,0:T(4,128)(2,1)S(1)} %get-tuple-element.51.refs_0_), channel_id=1, source_target_pairs={{0,1},{1,0},{2,3},{3,2},{4,5},{5,4},{6,7},{7,6},{8,9},{9,8},{10,11... | collective-permute-start | bytes 39944 | tf_op jit(solution)/shard_map/ppermute | solution.py:213
  40.6 3.2 %collective-permute-start.15 = (bf16[4,1,4,416]{3,2,1,0:T(4,128)(2,1)S(1)}, bf16[4,1,4,416]{3,2,1,0:T(4,128)(2,1)S(1)}, u32[]{:S(2)}, u32[]{:S(2)}) collective-permute-start(bf16[4,1,4,416]{3,2,1,0:T(4,128)(2,1)S(1)} %get-tuple-element.52), channel_id=1, source_target_pairs={{0,3},{1,2},{2,1},{3,0},{4,7},{5,6},{6,5},{7,4},{8,11},{9,10},{10,... | collective-permute-start | bytes 39944 | tf_op jit(solution)/shard_map/ppermute | solution.py:213
  42.2 3.7 %collective-permute-start.13 = (bf16[4,1,4,416]{3,2,1,0:T(4,128)(2,1)S(1)}, bf16[4,1,4,416]{3,2,1,0:T(4,128)(2,1)S(1)}, u32[]{:S(2)}, u32[]{:S(2)}) collective-permute-start(bf16[4,1,4,416]{3,2,1,0:T(4,128)(2,1)S(1)} %get-tuple-element.52), channel_id=1, source_target_pairs={{0,2},{2,0},{4,6},{6,4},{8,10},{10,8},{12,14},{14,12},{1,3},{3,1},... | collective-permute-start | bytes 39944 | tf_op jit(solution)/shard_map/ppermute | solution.py:194
  (17 other events, 136.9 us)

commit v3 on v2

--- a/solution.py
+++ b/solution.py
@@ -84,11 +84,11 @@
     sin_ref[...] = jnp.where(lane < half, -sin, sin)
 
 
-def digits(n):
+def digits(n, first=2):
     high = n.bit_length() - 1
     out = []
     while high:
-        low = max(high - 2, 0)
+        low = max(high - (2 if out else first), 0)
         out.append((low, 1 << (high - low)))
         high = low
     return out
@@ -105,13 +105,13 @@
         at += ref.shape[0]
 
 
-def part_shapes(n, rows, columns):
-    _, count = digits(n)[0]
+def part_shapes(n, rows, columns, first=2):
+    _, count = digits(n, first)[0]
     return (jax.ShapeDtypeStruct((1, n // count, rows, columns), BF16),) * count
 
 
-def exchange(parts, n, beside=(), other_core=False):
-    levels = digits(n)
+def exchange(parts, n, beside=(), other_core=False, first=2):
+    levels = digits(n, first)
     offsets = [0]
     for level, (shift, count) in enumerate(levels):
         last = level + 1 == len(levels)
@@ -147,7 +147,7 @@
 def place_blocks(target, at, layout, refs):
     for offsets, ref in zip(layout, refs):
         for i, offset in enumerate(offsets):
-            target[at ^ offset] = ref[i, 0].astype(F32)
+            target[at ^ offset, : ref.shape[2]] = ref[i, 0].astype(F32)
 
 
 def join_body(*refs):
@@ -158,11 +158,11 @@
         at += ref.shape[0]
 
 
-def digits(n):
+def digits(n, first=2):
     high = n.bit_length() - 1
     out = []
     while high:
-        low = max(high - 2, 0)
+        low = max(high - (2 if out else first), 0)
         out.append((low, 1 << (high - low)))
         high = low
     return out
@@ -179,13 +179,13 @@
         at += ref.shape[0]
 
 
-def part_shapes(n, rows, columns):
-    _, count = digits(n)[0]
+def part_shapes(n, rows, columns, first=2):
+    _, count = digits(n, first)[0]
     return (jax.ShapeDtypeStruct((1, n // count, rows, columns), BF16),) * count
 
 
-def exchange(parts, n, beside=(), other_core=False):
-    levels = digits(n)
+def exchange(parts, n, beside=(), other_core=False, first=2):
+    levels = digits(n, first)
     offsets = [0]
     for level, (shift, count) in enumerate(levels):
         last = level + 1 == len(levels)
@@ -221,7 +221,7 @@
 def place_blocks(target, at, layout, refs):
     for offsets, ref in zip(layout, refs):
         for i, offset in enumerate(offsets):
-            target[at ^ offset] = ref[i, 0].astype(F32)
+            target[at ^ offset, : ref.shape[2]] = ref[i, 0].astype(F32)
 
 
 def project_body(
@@ -278,7 +278,7 @@
     size = parts[0].shape[1]
     for i, part in enumerate(parts):
         for j in range(size):
-            part[0, j] = source[wide_at ^ (i * size + j)].astype(BF16)
+            part[0, j] = source[wide_at ^ (i * size + j), : part.shape[2]].astype(BF16)
 
 
 def mixer_body(dims, layout, out_count, length_ref, place, *refs):
@@ -293,12 +293,12 @@
     hs = HEAD_SIZE
     repeat = q_heads // kv_heads
     for i in range(feat.shape[0]):
-        fs[:, i * columns : (i + 1) * columns] = feat[i, :, :columns]
-        bc[:, i * shared : (i + 1) * shared] = feat[i, :, shared_at : shared_at + shared]
+        fs[:t_count, i * columns : (i + 1) * columns] = feat[i, :t_count, :columns]
+        bc[:t_count, i * shared : (i + 1) * shared] = feat[i, :t_count, shared_at : shared_at + shared]
     length = length_ref[0]
 
     turned = q_heads + kv_heads
-    stacked = jnp.concatenate([fs[:, h * hs : (h + 1) * hs] for h in range(turned)], axis=0)
+    stacked = jnp.concatenate([fs[:t_count, h * hs : (h + 1) * hs] for h in range(turned)], axis=0)
     cos = jnp.concatenate([cos_ref[...]] * turned, axis=0)
     sin = jnp.concatenate([sin_ref[...]] * turned, axis=0)
     swapped = jnp.concatenate([stacked[:, hs // 2 :], stacked[:, : hs // 2]], axis=1)
@@ -315,7 +315,7 @@
         at = q_heads * t_count + k * t_count
         new_keys = jnp.concatenate([rotated[at : at + t_count], filler], axis=0).astype(BF16)
         v_at = (turned + k) * hs
-        new_values = jnp.concatenate([fs[:, v_at : v_at + hs], filler], axis=0).astype(BF16)
+        new_values = jnp.concatenate([fs[:t_count, v_at : v_at + hs], filler], axis=0).astype(BF16)
         head = slice(k * hs, (k + 1) * hs)
         cache = jnp.where(live, dot_nt(queries, key_ref[:, head]) * scale, -1e30)
         fresh = jnp.where(causal, dot_nt(queries, new_keys) * scale, -1e30)
@@ -330,21 +330,23 @@
         )
         for r in range(repeat):
             h = k * repeat + r
-            own[:, h * hs : (h + 1) * hs] = attended[r * t_count : (r + 1) * t_count]
+            own[:t_count, h * hs : (h + 1) * hs] = attended[r * t_count : (r + 1) * t_count]
 
     x_at = (turned + kv_heads) * hs
     m_size = heads * head_width
     states = bc.shape[1] // 2
-    write = silu(bc[:, :states])
-    read = silu(bc[:, states:])
+    write = silu(bc[:t_count, :states])
+    read = silu(bc[:t_count, states:])
     read_high = read.astype(BF16)
     read_low = (read - read_high.astype(F32)).astype(BF16)
-    carried = dot_nt(read_high, state_ref[...]) + dot_nt(read_low, state_ref[...])
+    both = jnp.concatenate([read_high.astype(F32), read_low.astype(F32)], axis=0).astype(BF16)
+    both = dot_nt(both, state_ref[...])
+    carried = both[:t_count] + both[t_count:]
     count = heads * t_count
 
     def tall(v, at):
         return jnp.concatenate(
-            [v[:, at + h * head_width : at + (h + 1) * head_width] for h in range(heads)], axis=0
+            [v[:t_count, at + h * head_width : at + (h + 1) * head_width] for h in range(heads)], axis=0
         )
 
     row_head = lax.broadcasted_iota(jnp.int32, (count, heads), 0) // t_count
@@ -387,12 +389,12 @@
     m_at = q_heads * hs
     for h in range(heads):
         at = h * head_width
-        own[:, m_at + at : m_at + at + head_width] = (
+        own[:t_count, m_at + at : m_at + at + head_width] = (
             gated[h * t_count : (h + 1) * t_count] * gain_ref[:, at : at + head_width]
         )
     targets, _, piece = cut.shape
     for i in range(targets):
-        cut[i] = own[:, i * piece : (i + 1) * piece]
+        cut[i, :t_count] = own[:t_count, i * piece : (i + 1) * piece]
     spread_blocks(place[0], cut, parts)
 
 
@@ -489,7 +491,7 @@
 
     held = tokens[None]
     offsets = [0]
-    for shift, count in digits(n_wide):
+    for shift, count in digits(n_wide, 1):
         steps = [digit << shift for digit in range(1, count)]
         pieces = [held] + [
             lax.ppermute(held, "wide", [(j, j ^ step) for j in range(n_wide)]) for step in steps
@@ -536,7 +538,7 @@
     )
     *parts, inv, step_raw = call(
         functools.partial(combine_body, width * n_short, order),
-        part_shapes(n_wide, own_rows, used)
+        part_shapes(n_wide, own_rows, used, 1)
         + (
             jax.ShapeDtypeStruct((rows, LANES), F32),
             jax.ShapeDtypeStruct((own_rows, LANES), F32),
@@ -577,11 +579,12 @@
         )
         return made[1:]
 
-    features, layout = exchange(parts, n_wide, (gate, up))
+    features, layout = exchange(parts, n_wide, (gate, up), first=1)
     gate_own, up_own, ff_send = made
     features, ff_send = lax.optimization_barrier((features, ff_send))
     ff_received = lax.ppermute(ff_send, "short", other_core)
     out_shapes = part_shapes(n_wide, own_rows, piece)
+    full_rows = round_up(own_rows, 8)
     parts = call(
         functools.partial(
             mixer_body,
@@ -608,11 +611,11 @@
         ),
         [IN_SMEM] * 2 + [IN_VMEM] * (len(features) + 10) + [ANYWHERE],
         [
-            pltpu.VMEM((n_wide, own_rows, used), F32),
-            pltpu.VMEM((own_rows, n_wide * columns), F32),
-            pltpu.VMEM((own_rows, n_wide * shared), F32),
-            pltpu.VMEM((own_rows, n_wide * piece), F32),
-            pltpu.VMEM((n_wide, own_rows, piece), F32),
+            pltpu.VMEM((n_wide, full_rows, used), F32),
+            pltpu.VMEM((full_rows, n_wide * columns), F32),
+            pltpu.VMEM((full_rows, n_wide * shared), F32),
+            pltpu.VMEM((full_rows, n_wide * piece), F32),
+            pltpu.VMEM((n_wide, full_rows, piece), F32),
         ],
         flops=4 * own_rows * state_cache.size,
         nbytes=6 * state_cache.size,

time: 58.7 us -> 57.4 us (0.978)
  waiting for transfers between devices: 11.4 us -> 9.55 us
  starting transfers between devices: 19.7 us -> 20.3 us
    ppermute x4, waiting for transfers between devices: 5.17 us -> 3.54 us  [on_device(): lax.ppermute(held, 'wide', [(j, j ^ step) for j in range(n_wide)])]
    ppermute x8, starting transfers between devices: 10.9 us -> 11.7 us  [exchange(): lax.ppermute(part, 'wide', [(j, j ^ step) for j in range(n)])]
  transfers between devices with their start and end apart: 16 -> 16, of which waited for: 7 -> 7; matrix products, arithmetic and copies ran while one was open for 1% -> 1% of each run, Pallas kernels for 18% -> 19%
where the time goes in v3:
time: 57.4 us; the launch traced here: 57.1 us
  starting transfers between devices  20.3 us (35%)
  Pallas kernels  14.1 us (25%)
  blocking collectives  10.3 us (18%)
  waiting for transfers between devices  9.55 us (17%)
  local copies, waits for them, and re-layouts  1.08 us (2%)
  between operations  1.05 us (2%)
  other arithmetic  0.78 us (1%)
    pallas_call x12, Pallas kernels, call(): pl.pallas_call(body, out_shape=out_shape, in_specs=specs, out_specs=outs,...  14.1 us
    ppermute x8, starting transfers between devices, exchange(): lax.ppermute(part, 'wide', [(j, j ^ step) for j in range(n)])  11.7 us
    all_to_all x1, blocking collectives, on_device(): lax.all_to_all(summed, 'wide', split_axis=0, concat_axis=0, tiled=True)  10.3 us
    ppermute x4, starting transfers between devices, on_device(): lax.ppermute(held, 'wide', [(j, j ^ step) for j in range(n_wide)])  7.52 us
    ppermute x8, waiting for transfers between devices, exchange(): lax.ppermute(part, 'wide', [(j, j ^ step) for j in range(n)])  4.91 us
    ppermute x4, waiting for transfers between devices, on_device(): lax.ppermute(held, 'wide', [(j, j ^ step) for j in range(n_wide)])  3.54 us
  transfers between devices with their start and end apart: 16, of which 7 were waited for; matrix products, arithmetic and copies ran while one was open for 1% of the time, Pallas kernels for 19%

profile of v3, /device:TPU:0, one launch (start us, length us, event | category | flops | bytes accessed | tf_op | source)
XLA Modules:
  0.0 57.1 jit_solution(10437420813345927542)
XLA Ops:
  0.0 4.0 %collective-permute-start = (bf16[1,4,2560]{2,1,0:T(4,128)(2,1)}, bf16[1,4,2560]{2,1,0:T(4,128)(2,1)S(1)}, u32[]{:S(2)}, u32[]{:S(2)}) collective-permute-start(bf16[1,4,2560]{2,1,0:T(4,128)(2,1)} %bitcast.30), channel_id=1, source_target_pairs={{0,8},{2,10},{4,12},{6,14},{8,0},{10,2},{12,4},{14,6},{1,9},{3,11}... | collective-permute-start | bytes 61448 | tf_op jit(solution)/shard_map/ppermute | solution.py:497
  6.4 2.5 %collective-permute-start.3 = (bf16[2,4,2560]{2,1,0:T(4,128)(2,1)S(1)}, bf16[2,4,2560]{2,1,0:T(4,128)(2,1)S(1)}, u32[]{:S(2)}, u32[]{:S(2)}) collective-permute-start(bf16[2,4,2560]{2,1,0:T(4,128)(2,1)S(1)} %join.1.refs_0_), channel_id=1, source_target_pairs={{0,6},{2,4},{4,2},{6,0},{8,14},{10,12},{12,10},{14,8},{1,7},{3,5},... | collective-permute-start | bytes 122888 | tf_op jit(solution)/shard_map/ppermute | solution.py:497
  9.9 1.8 %collective-permute-done.3.refs_3_ = bf16[2,4,2560]{2,1,0:T(4,128)(2,1)S(1)} collective-permute-done((bf16[2,4,2560]{2,1,0:T(4,128)(2,1)S(1)}, bf16[2,4,2560]{2,1,0:T(4,128)(2,1)S(1)}, u32[]{:S(2)}, u32[]{:S(2)}) %collective-permute-start.3) | collective-permute-done | bytes 40992 | tf_op jit(solution)/shard_map/ppermute | solution.py:497
  11.7 1.2 %collective-permute-done.2.refs_2_ = bf16[2,4,2560]{2,1,0:T(4,128)(2,1)S(1)} collective-permute-done((bf16[2,4,2560]{2,1,0:T(4,128)(2,1)S(1)}, bf16[2,4,2560]{2,1,0:T(4,128)(2,1)S(1)}, u32[]{:S(2)}, u32[]{:S(2)}) %collective-permute-start.2) | collective-permute-done | bytes 40992 | tf_op jit(solution)/shard_map/ppermute | solution.py:497
  13.4 1.9 %project.1 = (bf16[32,2560]{1,0:T(8,128)(2,1)S(1)}, f32[32,1152]{1,0:T(8,128)S(1)}, f32[32,384]{1,0:T(8,128)S(1)}) custom-call(s32[2]{0:T(128)S(1)} %pad_add_fusion.place, f32[4,128]{1,0:T(4,128)S(1)} %get-tuple-element.31.refs_2_.after.refs_5_, bf16[2,4,2560]{2,1,0:T(4,128)(2,1)S(1)} %join.1.refs_0_, ...), custom_call_target="tpu_custom_call" | custom-call | flops 256901120 | bytes 160563200 | tf_op jit(solution)/shard_map/project/pallas_call | solution.py:62
  15.4 1.7 %own_group.1.keep_ref = f32[32,768]{1,0:T(8,128)S(1)} custom-call(s32[2]{0:T(128)S(1)} %pad_add_fusion.place, bf16[32,2560]{1,0:T(8,128)(2,1)S(1)} %get-tuple-element.32.xg_ref, bf16[2,736,2560]{2,1,0:T(8,128)(2,1)S(1)} %bitcast.16), custom_call_target="tpu_custom_call" | custom-call | flops 256901120 | bytes 4014080 | tf_op jit(solution)/shard_map/own_group/pallas_call | solution.py:62
  17.2 2.6 %collective-permute-start.5 = (bf16[1,4,4,896]{3,2,1,0:T(4,128)(2,1)S(1)}, bf16[1,4,4,896]{3,2,1,0:T(4,128)(2,1)S(1)}, u32[]{:S(2)}, u32[]{:S(2)}) collective-permute-start(bf16[1,4,4,896]{3,2,1,0:T(4,128)(2,1)S(1)} %get-tuple-element.36), channel_id=1, source_target_pairs={{0,8},{2,10},{4,12},{6,14},{8,0},{10,2},{12,4},{14,6},{1,9},{3,11}... | collective-permute-start | bytes 86024 | tf_op jit(solution)/shard_map/ppermute | solution.py:194
  19.9 2.1 %gate.1.refs_2_.gate_own_ref.gate_ref = f32[32,2688]{1,0:T(8,128)S(1)} custom-call(bf16[32,2560]{1,0:T(8,128)(2,1)S(1)} %get-tuple-element.32.xg_ref, f32[32,128]{1,0:T(8,128)S(1)} %get-tuple-element.37.inv_ref, bf16[2560,2688]{1,0:T(8,128)(2,1)S(1)} %bitcast.18), custom_call_target="tpu_custom_call" | custom-call | flops 440401920 | bytes 13762560 | tf_op jit(solution)/shard_map/gate/pallas_call | solution.py:62
  22.7 1.7 %collective-permute-start.7 = (bf16[2,1,4,896]{3,2,1,0:T(4,128)(2,1)S(1)}, bf16[2,1,4,896]{3,2,1,0:T(4,128)(2,1)S(1)}, u32[]{:S(2)}, u32[]{:S(2)}) collective-permute-start(bf16[2,1,4,896]{3,2,1,0:T(4,128)(2,1)S(1)} %get-tuple-element.40), channel_id=1, source_target_pairs={{0,4},{2,6},{4,0},{6,2},{8,12},{10,14},{12,8},{14,10},{1,5},{3,7},... | collective-permute-start | bytes 43016 | tf_op jit(solution)/shard_map/ppermute | solution.py:194
  24.4 1.3 %collective-permute-start.8 = (bf16[2,1,4,896]{3,2,1,0:T(4,128)(2,1)S(1)}, bf16[2,1,4,896]{3,2,1,0:T(4,128)(2,1)S(1)}, u32[]{:S(2)}, u32[]{:S(2)}) collective-permute-start(bf16[2,1,4,896]{3,2,1,0:T(4,128)(2,1)S(1)} %get-tuple-element.41), channel_id=1, source_target_pairs={{0,6},{2,4},{4,2},{6,0},{8,14},{10,12},{12,10},{14,8},{1,7},{3,5},... | collective-permute-start | bytes 43016 | tf_op jit(solution)/shard_map/ppermute | solution.py:194
  25.7 2.2 %up.1 = (f32[32,2688]{1,0:T(8,128)S(1)}, bf16[2,32,2688]{2,1,0:T(8,128)(2,1)S(1)}) custom-call(bf16[32,2560]{1,0:T(8,128)(2,1)S(1)} %get-tuple-element.32.xg_ref, f32[32,128]{1,0:T(8,128)S(1)} %get-tuple-element.37.inv_ref, bf16[2560,2688]{1,0:T(8,128)(2,1)S(1)} %bitcast.20, f32[32,2688]{1,0:T(8,128)S(1)} %gate.1.refs_2_.gate_own_ref.gate_ref, ...), custom_call_target="tpu_custom_call" | custom-call | flops 440401920 | bytes 13762560 | tf_op jit(solution)/shard_map/up/pallas_call | solution.py:62
  27.9 1.1 %collective-permute-done.8.refs_3_ = bf16[2,1,4,896]{3,2,1,0:T(4,128)(2,1)S(1)} collective-permute-done((bf16[2,1,4,896]{3,2,1,0:T(4,128)(2,1)S(1)}, bf16[2,1,4,896]{3,2,1,0:T(4,128)(2,1)S(1)}, u32[]{:S(2)}, u32[]{:S(2)}) %collective-permute-start.8) | collective-permute-done | bytes 14368 | tf_op jit(solution)/shard_map/ppermute | solution.py:194
  29.1 2.0 %mixers.1 = (bf16[1,2,4,416]{3,2,1,0:T(4,128)(2,1)S(1)}, bf16[1,2,4,416]{3,2,1,0:T(4,128)(2,1)S(1)}, bf16[1,2,4,416]{3,2,1,0:T(4,128)(2,1)S(1)}, bf16[1,2,4,416]{3,2,1,0:T(4,128)(2,1)S(1)}) custom-call(s32[1]{0:T(128)S(6)} %copy.18.length_ref, s32[2]{0:T(128)S(1)} %pad_add_fusion.place, bf16[2,1,4,896]{3,2,1,0:T(4,128)(2,1)S(1)} %get-tuple-element.43.after_ref.refs_0_, ...), custom_call_target="tpu_custom_call" | custom-call | flops 8388608 | bytes 3145728 | tf_op jit(solution)/shard_map/mixers/pallas_call | solution.py:62
  31.1 0.8 %collective-permute-start.9 = (bf16[1,2,4,416]{3,2,1,0:T(4,128)(2,1)S(1)}, bf16[1,2,4,416]{3,2,1,0:T(4,128)(2,1)S(1)}, u32[]{:S(2)}, u32[]{:S(2)}) collective-permute-start(bf16[1,2,4,416]{3,2,1,0:T(4,128)(2,1)S(1)} %get-tuple-element.51), channel_id=1, source_target_pairs={{0,4},{2,6},{4,0},{6,2},{8,12},{10,14},{12,8},{14,10},{1,5},{3,7},... | collective-permute-start | bytes 19976 | tf_op jit(solution)/shard_map/ppermute | solution.py:194
  31.8 2.6 %collective-permute-start.10 = (bf16[1,2,4,416]{3,2,1,0:T(4,128)(2,1)S(1)}, bf16[1,2,4,416]{3,2,1,0:T(4,128)(2,1)S(1)}, u32[]{:S(2)}, u32[]{:S(2)}) collective-permute-start(bf16[1,2,4,416]{3,2,1,0:T(4,128)(2,1)S(1)} %get-tuple-element.52), channel_id=1, source_target_pairs={{0,8},{2,10},{4,12},{6,14},{8,0},{10,2},{12,4},{14,6},{1,9},{3,11}... | collective-permute-start | bytes 19976 | tf_op jit(solution)/shard_map/ppermute | solution.py:194
  34.4 1.1 %collective-permute-start.11 = (bf16[1,2,4,416]{3,2,1,0:T(4,128)(2,1)S(1)}, bf16[1,2,4,416]{3,2,1,0:T(4,128)(2,1)S(1)}, u32[]{:S(2)}, u32[]{:S(2)}) collective-permute-start(bf16[1,2,4,416]{3,2,1,0:T(4,128)(2,1)S(1)} %get-tuple-element.53), channel_id=1, source_target_pairs={{0,12},{2,14},{4,8},{6,10},{8,4},{10,6},{12,0},{14,2},{1,13},{3,15... | collective-permute-start | bytes 19976 | tf_op jit(solution)/shard_map/ppermute | solution.py:194
  35.6 2.0 %down.1.refs_4_.refs_5_ = f32[32,2560]{1,0:T(8,128)S(1)} custom-call(f32[32,2688]{1,0:T(8,128)S(1)} %gate.1.refs_2_.gate_own_ref.gate_ref, f32[32,2688]{1,0:T(8,128)S(1)} %get-tuple-element.49.refs_14_.up_ref, bf16[2,32,2688]{2,1,0:T(8,128)(2,1)S(1)} %collective-permute-done.12.recv_ref, bf16[2688,2560]{1,0:T(8,128)(2,1)S(1)} %bitcast.22, ...), custom_call_target="tpu_custom_call" | custom-call | flops 440401920 | bytes 13762560 | tf_op jit(solution)/shard_map/down/pallas_call | solution.py:62
  37.6 2.3 %collective-permute-done.11.refs_3_ = bf16[1,2,4,416]{3,2,1,0:T(4,128)(2,1)S(1)} collective-permute-done((bf16[1,2,4,416]{3,2,1,0:T(4,128)(2,1)S(1)}, bf16[1,2,4,416]{3,2,1,0:T(4,128)(2,1)S(1)}, u32[]{:S(2)}, u32[]{:S(2)}) %collective-permute-start.11) | collective-permute-done | bytes 6688 | tf_op jit(solution)/shard_map/ppermute | solution.py:194
  39.9 1.0 %collective-permute-start.15 = (bf16[4,1,4,416]{3,2,1,0:T(4,128)(2,1)S(1)}, bf16[4,1,4,416]{3,2,1,0:T(4,128)(2,1)S(1)}, u32[]{:S(2)}, u32[]{:S(2)}) collective-permute-start(bf16[4,1,4,416]{3,2,1,0:T(4,128)(2,1)S(1)} %get-tuple-element.56), channel_id=1, source_target_pairs={{0,3},{1,2},{2,1},{3,0},{4,7},{5,6},{6,5},{7,4},{8,11},{9,10},{10,... | collective-permute-start | bytes 39944 | tf_op jit(solution)/shard_map/ppermute | solution.py:213
  41.0 1.1 %collective-permute-start.13 = (bf16[4,1,4,416]{3,2,1,0:T(4,128)(2,1)S(1)}, bf16[4,1,4,416]{3,2,1,0:T(4,128)(2,1)S(1)}, u32[]{:S(2)}, u32[]{:S(2)}) collective-permute-start(bf16[4,1,4,416]{3,2,1,0:T(4,128)(2,1)S(1)} %get-tuple-element.56), channel_id=1, source_target_pairs={{0,2},{2,0},{4,6},{6,4},{8,10},{10,8},{12,14},{14,12},{1,3},{3,1},... | collective-permute-start | bytes 39944 | tf_op jit(solution)/shard_map/ppermute | solution.py:194
  42.0 1.1 %collective-permute-done.15.refs_3_ = bf16[4,1,4,416]{3,2,1,0:T(4,128)(2,1)S(1)} collective-permute-done((bf16[4,1,4,416]{3,2,1,0:T(4,128)(2,1)S(1)}, bf16[4,1,4,416]{3,2,1,0:T(4,128)(2,1)S(1)}, u32[]{:S(2)}, u32[]{:S(2)}) %collective-permute-start.15) | collective-permute-done | bytes 13344 | tf_op jit(solution)/shard_map/ppermute | solution.py:213
  43.1 1.6 %collective-permute-done.13.refs_1_ = bf16[4,1,4,416]{3,2,1,0:T(4,128)(2,1)S(1)} collective-permute-done((bf16[4,1,4,416]{3,2,1,0:T(4,128)(2,1)S(1)}, bf16[4,1,4,416]{3,2,1,0:T(4,128)(2,1)S(1)}, u32[]{:S(2)}, u32[]{:S(2)}) %collective-permute-start.13) | collective-permute-done | bytes 13344 | tf_op jit(solution)/shard_map/ppermute | solution.py:194
  44.7 1.4 %output.1 = bf16[8,4,2560]{2,1,0:T(4,128)(2,1)S(1)} custom-call(s32[2]{0:T(128)S(1)} %pad_add_fusion.place, bf16[4,1,4,416]{3,2,1,0:T(4,128)(2,1)S(1)} %get-tuple-element.55.refs_0_, bf16[4,1,4,416]{3,2,1,0:T(4,128)(2,1)S(1)} %collective-permute-done.13.refs_1_, bf16[4,1,4,416]{3,2,1,0:T(4,128)(2,1)S(1)} %collective-permute-done.14.refs_2_, ...), custom_call_target="tpu_custom_call" | custom-call | flops 136314880 | bytes 4259840 | tf_op jit(solution)/shard_map/output/pallas_call | solution.py:62
  46.1 10.3 %all_to_all.5 = bf16[8,4,2560]{2,1,0:T(4,128)(2,1)S(1)} all-to-all(bf16[8,4,2560]{2,1,0:T(4,128)(2,1)S(1)} %output.1), channel_id=1, replica_groups=mesh['groups'=2,'wide'=8,'short'=2] {'wide'}, dimensions={0} | all-to-all | bytes 327680 | tf_op jit(solution)/shard_map/all_to_all | solution.py:651
  (79 shorter events, 4.8 us)
Async XLA Ops:
  0.0 6.1 %collective-permute-start = (bf16[1,4,2560]{2,1,0:T(4,128)(2,1)}, bf16[1,4,2560]{2,1,0:T(4,128)(2,1)S(1)}, u32[]{:S(2)}, u32[]{:S(2)}) collective-permute-start(bf16[1,4,2560]{2,1,0:T(4,128)(2,1)} %bitcast.30), channel_id=1, source_target_pairs={{0,8},{2,10},{4,12},{6,14},{8,0},{10,2},{12,4},{14,6},{1,9},{3,11}... | collective-permute-start | bytes 61448 | tf_op jit(solution)/shard_map/ppermute | solution.py:497
  5.4 14.4 %slice-start = ((s8[13762560]{0:T(1024)(128)(4,1)}), s8[4194304]{0:T(1024)(128)(4,1)S(1)}, s32[]{:S(2)}) async-start(s8[13762560]{0:T(1024)(128)(4,1)} %bitcast.17), calls=%async_computation.1 | async-start | bytes 8388608
  5.5 14.3 %slice-start.1 = ((s8[13762560]{0:T(1024)(128)(4,1)}), s8[4194304]{0:T(1024)(128)(4,1)S(1)}, s32[]{:S(2)}) async-start(s8[13762560]{0:T(1024)(128)(4,1)} %bitcast.17), calls=%async_computation.2 | async-start | bytes 8388608
  5.5 14.3 %slice-start.2 = ((s8[13762560]{0:T(1024)(128)(4,1)}), s8[4194304]{0:T(1024)(128)(4,1)S(1)}, s32[]{:S(2)}) async-start(s8[13762560]{0:T(1024)(128)(4,1)} %bitcast.17), calls=%async_computation.3 | async-start | bytes 8388608
  5.5 14.3 %slice-start.3 = ((s8[13762560]{0:T(1024)(128)(4,1)}), s8[1179648]{0:T(1024)(128)(4,1)S(1)}, s32[]{:S(2)}) async-start(s8[13762560]{0:T(1024)(128)(4,1)} %bitcast.17), calls=%async_computation.4 | async-start | bytes 2359296
  6.4 5.3 %collective-permute-start.3 = (bf16[2,4,2560]{2,1,0:T(4,128)(2,1)S(1)}, bf16[2,4,2560]{2,1,0:T(4,128)(2,1)S(1)}, u32[]{:S(2)}, u32[]{:S(2)}) collective-permute-start(bf16[2,4,2560]{2,1,0:T(4,128)(2,1)S(1)} %join.1.refs_0_), channel_id=1, source_target_pairs={{0,6},{2,4},{4,2},{6,0},{8,14},{10,12},{12,10},{14,8},{1,7},{3,5},... | collective-permute-start | bytes 122888 | tf_op jit(solution)/shard_map/ppermute | solution.py:497
  8.9 4.0 %collective-permute-start.2 = (bf16[2,4,2560]{2,1,0:T(4,128)(2,1)S(1)}, bf16[2,4,2560]{2,1,0:T(4,128)(2,1)S(1)}, u32[]{:S(2)}, u32[]{:S(2)}) collective-permute-start(bf16[2,4,2560]{2,1,0:T(4,128)(2,1)S(1)} %join.1.refs_0_), channel_id=1, source_target_pairs={{0,4},{2,6},{4,0},{6,2},{8,12},{10,14},{12,8},{14,10},{1,5},{3,7},... | collective-permute-start | bytes 122888 | tf_op jit(solution)/shard_map/ppermute | solution.py:497
  9.4 4.0 %collective-permute-start.1 = (bf16[2,4,2560]{2,1,0:T(4,128)(2,1)S(1)}, bf16[2,4,2560]{2,1,0:T(4,128)(2,1)S(1)}, u32[]{:S(2)}, u32[]{:S(2)}) collective-permute-start(bf16[2,4,2560]{2,1,0:T(4,128)(2,1)S(1)} %join.1.refs_0_), channel_id=1, source_target_pairs={{0,2},{2,0},{4,6},{6,4},{8,10},{10,8},{12,14},{14,12},{1,3},{3,1},... | collective-permute-start | bytes 122888 | tf_op jit(solution)/shard_map/ppermute | solution.py:497
  15.3 1.8 %collective-permute-start.4 = (f32[32,1152]{1,0:T(8,128)S(1)}, f32[32,1152]{1,0:T(8,128)S(1)}, u32[]{:S(2)}, u32[]{:S(2)}) collective-permute-start(f32[32,1152]{1,0:T(8,128)S(1)} %get-tuple-element.34), channel_id=1, source_target_pairs={{0,1},{1,0},{2,3},{3,2},{4,5},{5,4},{6,7},{7,6},{8,9},{9,8},{10,11... | collective-permute-start | bytes 442376 | tf_op jit(solution)/shard_map/ppermute | solution.py:529
  17.2 4.9 %collective-permute-start.5 = (bf16[1,4,4,896]{3,2,1,0:T(4,128)(2,1)S(1)}, bf16[1,4,4,896]{3,2,1,0:T(4,128)(2,1)S(1)}, u32[]{:S(2)}, u32[]{:S(2)}) collective-permute-start(bf16[1,4,4,896]{3,2,1,0:T(4,128)(2,1)S(1)} %get-tuple-element.36), channel_id=1, source_target_pairs={{0,8},{2,10},{4,12},{6,14},{8,0},{10,2},{12,4},{14,6},{1,9},{3,11}... | collective-permute-start | bytes 86024 | tf_op jit(solution)/shard_map/ppermute | solution.py:194
  19.9 15.6 %slice-start.8 = ((s8[13762560]{0:T(1024)(128)(4,1)}), s8[4194304]{0:T(1024)(128)(4,1)S(1)}, s32[]{:S(2)}) async-start(s8[13762560]{0:T(1024)(128)(4,1)} %bitcast.21), calls=%async_computation.9 | async-start | bytes 8388608
  19.9 15.6 %slice-start.9 = ((s8[13762560]{0:T(1024)(128)(4,1)}), s8[4194304]{0:T(1024)(128)(4,1)S(1)}, s32[]{:S(2)}) async-start(s8[13762560]{0:T(1024)(128)(4,1)} %bitcast.21), calls=%async_computation.10 | async-start | bytes 8388608
  22.1 5.8 %collective-permute-start.6 = (bf16[2,1,4,896]{3,2,1,0:T(4,128)(2,1)S(1)}, bf16[2,1,4,896]{3,2,1,0:T(4,128)(2,1)S(1)}, u32[]{:S(2)}, u32[]{:S(2)}) collective-permute-start(bf16[2,1,4,896]{3,2,1,0:T(4,128)(2,1)S(1)} %get-tuple-element.39), channel_id=1, source_target_pairs={{0,2},{2,0},{4,6},{6,4},{8,10},{10,8},{12,14},{14,12},{1,3},{3,1},... | collective-permute-start | bytes 43016 | tf_op jit(solution)/shard_map/ppermute | solution.py:194
  22.7 5.2 %collective-permute-start.7 = (bf16[2,1,4,896]{3,2,1,0:T(4,128)(2,1)S(1)}, bf16[2,1,4,896]{3,2,1,0:T(4,128)(2,1)S(1)}, u32[]{:S(2)}, u32[]{:S(2)}) collective-permute-start(bf16[2,1,4,896]{3,2,1,0:T(4,128)(2,1)S(1)} %get-tuple-element.40), channel_id=1, source_target_pairs={{0,4},{2,6},{4,0},{6,2},{8,12},{10,14},{12,8},{14,10},{1,5},{3,7},... | collective-permute-start | bytes 43016 | tf_op jit(solution)/shard_map/ppermute | solution.py:194
  24.4 4.6 %collective-permute-start.8 = (bf16[2,1,4,896]{3,2,1,0:T(4,128)(2,1)S(1)}, bf16[2,1,4,896]{3,2,1,0:T(4,128)(2,1)S(1)}, u32[]{:S(2)}, u32[]{:S(2)}) collective-permute-start(bf16[2,1,4,896]{3,2,1,0:T(4,128)(2,1)S(1)} %get-tuple-element.41), channel_id=1, source_target_pairs={{0,6},{2,4},{4,2},{6,0},{8,14},{10,12},{12,10},{14,8},{1,7},{3,5},... | collective-permute-start | bytes 43016 | tf_op jit(solution)/shard_map/ppermute | solution.py:194
  25.7 19.0 %slice-start.12 = ((s8[4259840]{0:T(1024)(128)(4,1)}), s8[4194304]{0:T(1024)(128)(4,1)S(1)}, s32[]{:S(2)}) async-start(s8[4259840]{0:T(1024)(128)(4,1)} %bitcast.23), calls=%async_computation.13 | async-start | bytes 8388608
  29.0 6.5 %collective-permute-start.12 = (bf16[2,32,2688]{2,1,0:T(8,128)(2,1)S(1)}, bf16[2,32,2688]{2,1,0:T(8,128)(2,1)S(1)}, u32[]{:S(2)}, u32[]{:S(2)}) collective-permute-start(bf16[2,32,2688]{2,1,0:T(8,128)(2,1)S(1)} %get-tuple-element.54), channel_id=1, source_target_pairs={{0,1},{1,0},{2,3},{3,2},{4,5},{5,4},{6,7},{7,6},{8,9},{9,8},{10,11... | collective-permute-start | bytes 1032200 | tf_op jit(solution)/shard_map/ppermute | solution.py:585
  29.1 15.6 %slice-start.13 = ((s8[4259840]{0:T(1024)(128)(4,1)}), s8[65536]{0:T(1024)(128)(4,1)S(1)}, s32[]{:S(2)}) async-start(s8[4259840]{0:T(1024)(128)(4,1)} %bitcast.23), calls=%async_computation.14 | async-start | bytes 131072
  31.1 6.5 %collective-permute-start.9 = (bf16[1,2,4,416]{3,2,1,0:T(4,128)(2,1)S(1)}, bf16[1,2,4,416]{3,2,1,0:T(4,128)(2,1)S(1)}, u32[]{:S(2)}, u32[]{:S(2)}) collective-permute-start(bf16[1,2,4,416]{3,2,1,0:T(4,128)(2,1)S(1)} %get-tuple-element.51), channel_id=1, source_target_pairs={{0,4},{2,6},{4,0},{6,2},{8,12},{10,14},{12,8},{14,10},{1,5},{3,7},... | collective-permute-start | bytes 19976 | tf_op jit(solution)/shard_map/ppermute | solution.py:194
  31.8 5.8 %collective-permute-start.10 = (bf16[1,2,4,416]{3,2,1,0:T(4,128)(2,1)S(1)}, bf16[1,2,4,416]{3,2,1,0:T(4,128)(2,1)S(1)}, u32[]{:S(2)}, u32[]{:S(2)}) collective-permute-start(bf16[1,2,4,416]{3,2,1,0:T(4,128)(2,1)S(1)} %get-tuple-element.52), channel_id=1, source_target_pairs={{0,8},{2,10},{4,12},{6,14},{8,0},{10,2},{12,4},{14,6},{1,9},{3,11}... | collective-permute-start | bytes 19976 | tf_op jit(solution)/shard_map/ppermute | solution.py:194
  34.4 5.4 %collective-permute-start.11 = (bf16[1,2,4,416]{3,2,1,0:T(4,128)(2,1)S(1)}, bf16[1,2,4,416]{3,2,1,0:T(4,128)(2,1)S(1)}, u32[]{:S(2)}, u32[]{:S(2)}) collective-permute-start(bf16[1,2,4,416]{3,2,1,0:T(4,128)(2,1)S(1)} %get-tuple-element.53), channel_id=1, source_target_pairs={{0,12},{2,14},{4,8},{6,10},{8,4},{10,6},{12,0},{14,2},{1,13},{3,15... | collective-permute-start | bytes 19976 | tf_op jit(solution)/shard_map/ppermute | solution.py:194
  39.9 2.1 %collective-permute-start.14 = (bf16[4,1,4,416]{3,2,1,0:T(4,128)(2,1)S(1)}, bf16[4,1,4,416]{3,2,1,0:T(4,128)(2,1)S(1)}, u32[]{:S(2)}, u32[]{:S(2)}) collective-permute-start(bf16[4,1,4,416]{3,2,1,0:T(4,128)(2,1)S(1)} %get-tuple-element.55.refs_0_), channel_id=1, source_target_pairs={{0,1},{1,0},{2,3},{3,2},{4,5},{5,4},{6,7},{7,6},{8,9},{9,8},{10,11... | collective-permute-start | bytes 39944 | tf_op jit(solution)/shard_map/ppermute | solution.py:213
  39.9 3.2 %collective-permute-start.15 = (bf16[4,1,4,416]{3,2,1,0:T(4,128)(2,1)S(1)}, bf16[4,1,4,416]{3,2,1,0:T(4,128)(2,1)S(1)}, u32[]{:S(2)}, u32[]{:S(2)}) collective-permute-start(bf16[4,1,4,416]{3,2,1,0:T(4,128)(2,1)S(1)} %get-tuple-element.56), channel_id=1, source_target_pairs={{0,3},{1,2},{2,1},{3,0},{4,7},{5,6},{6,5},{7,4},{8,11},{9,10},{10,... | collective-permute-start | bytes 39944 | tf_op jit(solution)/shard_map/ppermute | solution.py:213
  41.0 3.7 %collective-permute-start.13 = (bf16[4,1,4,416]{3,2,1,0:T(4,128)(2,1)S(1)}, bf16[4,1,4,416]{3,2,1,0:T(4,128)(2,1)S(1)}, u32[]{:S(2)}, u32[]{:S(2)}) collective-permute-start(bf16[4,1,4,416]{3,2,1,0:T(4,128)(2,1)S(1)} %get-tuple-element.56), channel_id=1, source_target_pairs={{0,2},{2,0},{4,6},{6,4},{8,10},{10,8},{12,14},{14,12},{1,3},{3,1},... | collective-permute-start | bytes 39944 | tf_op jit(solution)/shard_map/ppermute | solution.py:194
  (17 other events, 149.3 us)
